TPU v7x, 128 devices: a whole 4x4x4 slice. The times are simulated.
128 devices in a mesh: dp: 16 (over z, x), row: 2 (over y_hi), col: 4 (over y_lo, core).
Axes of the slice: x: 4, y: 4 (y_hi: 2, y_lo: 2; y = y_hi * 2 + y_lo), z: 4, core: 2. Of those that a mesh axis runs over, the one named last changes fastest.
Arguments:
- hidden_in: bfloat16 [16384, 960], P(('dp', 'col')), may hold values from -6 to 6
- segment_ids: int32 [16384], P(('dp', 'col')), may hold values from 0 to 2, as said below
- attn_gain: float32 [960], replicated, may hold values from 0.1 to 1.9
- q_weight: bfloat16 [960, 960], P('row', 'col'), may hold values from -0.1875 to 0.1875
- k_weight: bfloat16 [960, 320], P('row', 'col'), may hold values from -0.1875 to 0.1875
- v_weight: bfloat16 [960, 320], P('row', 'col'), may hold values from -0.1875 to 0.1875
- o_weight: bfloat16 [960, 960], P('row', 'col'), may hold values from -3.5 to 3.5
- ffn_gain: float32 [960], replicated, may hold values from 0.1 to 1.9
- gate_weight: bfloat16 [960, 2560], P('row', 'col'), may hold values from -0.1875 to 0.1875
- up_weight: bfloat16 [960, 2560], P('row', 'col'), may hold values from -0.1875 to 0.1875
- down_weight: bfloat16 [2560, 960], P('row', 'col'), may hold values from -0.125 to 0.125
- d_out: bfloat16 [16384, 960], P(('dp', 'col')), may hold values from -6 to 6
Outputs:
- block_out: float32 [16384, 960], P(('dp', 'col'))
- input_grad: float32 [16384, 960], P(('dp', 'col'))
- attn_gain_grad: float32 [960], replicated
- q_grad: float32 [960, 960], P('row', 'col')
- k_grad: float32 [960, 320], P('row', 'col')
- v_grad: float32 [960, 320], P('row', 'col')
- o_grad: float32 [960, 960], P('row', 'col')
- ffn_gain_grad: float32 [960], replicated
- gate_grad: float32 [960, 2560], P('row', 'col')
- up_grad: float32 [960, 2560], P('row', 'col')
- down_grad: float32 [2560, 960], P('row', 'col')
Inputs may be any that keep to these rules, and one draw needn't show every extreme that they name: `segment_ids`: within each sequence of 1024 consecutive tokens the ids never fall, start at 0 and take the values 0, 1 and 2; document 0 holds 204 to 255 tokens, document 2 ends the sequence with 1 to 256 tokens.
All inputs are finite; a program needn't handle non-finite values.
Results may differ from a plain program's by a relative error of at most 0.025.
Values may be sent and summed in bfloat16 or wider, within the bound.
A program may use at most 128 MiB of HBM per device.

v0:
```python
import jax
import jax.numpy as jnp
from jax import lax
from jax.sharding import PartitionSpec as P

HEADS = 15
KV_HEADS = 5
HEAD_DIM = 64


norm_eps = 1e-05
rope_base = 100000.0


def rounded(values):
    return lax.optimization_barrier(values.astype(jnp.bfloat16)).astype(jnp.float32)


def normalize(values, gain_vec):
    inverse = lax.rsqrt(jnp.mean(values * values, axis=1, keepdims=True) + norm_eps)
    unit_rows = values * inverse
    return ((unit_rows * gain_vec).astype(jnp.bfloat16), unit_rows, inverse)


def norm_back(gradient, unit_rows, inverse, gain_vec):
    scaled = gradient * gain_vec
    inner_sum = jnp.mean(scaled * unit_rows, axis=1, keepdims=True)
    return (inverse * (scaled - unit_rows * inner_sum), jnp.sum(gradient * unit_rows, axis=0))


def rotate(values, places, turn_sign):
    half_dim = values.shape[-1] // 2
    frequency = rope_base ** (-jnp.arange(half_dim, dtype=jnp.float32) * 2.0 / values.shape[-1])
    angles = places.astype(jnp.float32)[:, None] * frequency[None, :]
    cosine = jnp.cos(angles)[:, None, :]
    sine_part = turn_sign * jnp.sin(angles)[:, None, :]
    first_half = values[..., :half_dim]
    second_half = values[..., half_dim:]
    return jnp.concatenate(
        [
            first_half * cosine - second_half * sine_part,
            second_half * cosine + first_half * sine_part,
        ],
        axis=-1,
    )


def forward_project(inputs, weight_block):
    width_in = weight_block.shape[0]
    row_pos = lax.axis_index("row")
    row_slab = lax.dynamic_slice_in_dim(inputs, row_pos * width_in, width_in, 1)
    gathered = lax.all_gather(row_slab, "col", axis=0, tiled=True)
    partial_out = jnp.dot(gathered, weight_block, preferred_element_type=jnp.float32)
    arrived = lax.all_to_all(partial_out, "col", split_axis=0, concat_axis=1, tiled=True)
    result = lax.psum(arrived, "row")
    return (result, gathered)


def backward_project(gradient, weight_block, gathered):
    grad_cols = lax.all_to_all(gradient, "col", split_axis=1, concat_axis=0, tiled=True)
    weight_grad = lax.dot_general(
        gathered, grad_cols, (((0,), (0,)), ((), ())), preferred_element_type=jnp.float32
    )
    share_half = lax.psum_scatter(
        lax.dot_general(
            grad_cols, weight_block, (((1,), (1,)), ((), ())), preferred_element_type=jnp.float32
        ).astype(jnp.bfloat16),
        "col",
        scatter_dimension=0,
        tiled=True,
    ).astype(jnp.float32)
    joined = lax.all_gather(share_half.astype(jnp.bfloat16), "row", axis=1, tiled=True).astype(
        share_half.dtype
    )
    return (joined, weight_grad)


def scores_of(queries, keys_all, allowed, scaling):
    raw_scores = (
        jnp.einsum("qkgd,pkd->kgqp", queries, keys_all, preferred_element_type=jnp.float32)
        * scaling
    )
    return jnp.where(allowed, raw_scores, -jnp.inf)


def shards(
    hidden_in,
    segment_ids,
    attn_gain,
    q_weight,
    k_weight,
    v_weight,
    o_weight,
    ffn_gain,
    gate_weight,
    up_weight,
    down_weight,
    d_out,
):
    groups = lax.axis_size("col")
    rows_here = hidden_in.shape[0]
    seq_rows = rows_here * groups
    col_pos = lax.axis_index("col")
    q_cols = q_weight.shape[1]
    kv_cols = k_weight.shape[1]
    ff_cols = gate_weight.shape[1]
    share_heads = HEADS // KV_HEADS
    scaling = HEAD_DIM ** (-0.5)
    docs_all = lax.all_gather(segment_ids, "col", axis=0, tiled=True)
    query_index = col_pos * rows_here + jnp.arange(rows_here, dtype=jnp.int32)
    earlier = jnp.sum((docs_all[None, :] < segment_ids[:, None]).astype(jnp.int32), axis=1)
    places = query_index - earlier
    allowed = (segment_ids[:, None] == docs_all[None, :]) & (
        jnp.arange(seq_rows, dtype=jnp.int32)[None, :] <= query_index[:, None]
    )
    tokens = hidden_in.astype(jnp.float32)
    normed_one, unit_one, inverse_one = normalize(tokens, attn_gain)
    qkv_block = jnp.concatenate([q_weight, k_weight, v_weight], axis=1)
    qkv_rows, normed_one_cols = forward_project(normed_one, qkv_block)
    qkv_rows = rounded(qkv_rows).reshape(rows_here, groups, q_cols + 2 * kv_cols)
    query_rows = qkv_rows[:, :, :q_cols].reshape(rows_here, HEADS, HEAD_DIM)
    key_rows = qkv_rows[:, :, q_cols : q_cols + kv_cols].reshape(rows_here, KV_HEADS, HEAD_DIM)
    value_rows = (
        qkv_rows[:, :, q_cols + kv_cols :]
        .reshape(rows_here, KV_HEADS * HEAD_DIM)
        .astype(jnp.bfloat16)
    )
    queries = (
        rotate(query_rows, places, 1.0)
        .astype(jnp.bfloat16)
        .reshape(rows_here, KV_HEADS, share_heads, HEAD_DIM)
    )
    key_turned = (
        rotate(key_rows, places, 1.0).astype(jnp.bfloat16).reshape(rows_here, KV_HEADS * HEAD_DIM)
    )
    keys_all, values_all = (
        lax.all_gather(key_turned, "col", axis=0, tiled=True),
        lax.all_gather(value_rows, "col", axis=0, tiled=True),
    )
    keys_all = keys_all.reshape(seq_rows, KV_HEADS, HEAD_DIM)
    values_all = values_all.reshape(seq_rows, KV_HEADS, HEAD_DIM)
    scores = scores_of(queries, keys_all, allowed, scaling)
    row_top = jnp.max(scores, axis=-1, keepdims=True)
    exp_terms = jnp.exp(scores - row_top)
    exp_total = jnp.sum(exp_terms, axis=-1, keepdims=True)
    log_total = row_top + jnp.log(exp_total)
    attended = jnp.einsum(
        "kgqp,pkd->qkgd",
        (exp_terms / exp_total).astype(jnp.bfloat16),
        values_all,
        preferred_element_type=jnp.float32,
    )
    attn_rows = attended.reshape(rows_here, HEADS * HEAD_DIM).astype(jnp.bfloat16)
    attn_out, attn_rows_cols = forward_project(attn_rows, o_weight)
    middle = tokens + attn_out
    normed_two, unit_two, inverse_two = normalize(middle, ffn_gain)
    gate_up_block = jnp.concatenate([gate_weight, up_weight], axis=1)
    gate_up, normed_two_cols = forward_project(normed_two, gate_up_block)
    gate_up = rounded(gate_up).reshape(rows_here, groups, 2 * ff_cols)
    gate_vals = gate_up[:, :, :ff_cols].reshape(rows_here, groups * ff_cols)
    up_vals = gate_up[:, :, ff_cols:].reshape(rows_here, groups * ff_cols)
    sig_gate = jax.nn.sigmoid(gate_vals)
    silu_gate = gate_vals * sig_gate
    hidden_mid = (silu_gate * up_vals).astype(jnp.bfloat16)
    ffn_out, hidden_mid_cols = forward_project(hidden_mid, down_weight)
    block_out = middle + ffn_out
    d_hidden, down_grad = backward_project(d_out, down_weight, hidden_mid_cols)
    d_gate = d_hidden * up_vals * sig_gate * (1.0 + gate_vals * (1.0 - sig_gate))
    d_up = d_hidden * silu_gate
    d_gate_up = jnp.concatenate(
        [d_gate.reshape(rows_here, groups, ff_cols), d_up.reshape(rows_here, groups, ff_cols)],
        axis=2,
    )
    d_gate_up = d_gate_up.reshape(rows_here, 2 * groups * ff_cols).astype(jnp.bfloat16)
    d_normed_two, gate_up_grad = backward_project(d_gate_up, gate_up_block, normed_two_cols)
    d_middle, ffn_gain_part = norm_back(d_normed_two, unit_two, inverse_two, ffn_gain)
    d_middle = d_middle + d_out.astype(jnp.float32)
    d_attn, o_grad = backward_project(d_middle.astype(jnp.bfloat16), o_weight, attn_rows_cols)
    d_attn = d_attn.astype(jnp.bfloat16).reshape(rows_here, KV_HEADS, share_heads, HEAD_DIM)
    probs_again = jnp.exp(scores_of(queries, keys_all, allowed, scaling) - log_total)
    d_probs = jnp.einsum("qkgd,pkd->kgqp", d_attn, values_all, preferred_element_type=jnp.float32)
    inner_sum = jnp.sum(probs_again * d_probs, axis=-1, keepdims=True)
    d_scores = (probs_again * (d_probs - inner_sum)).astype(jnp.bfloat16)
    d_queries = (
        jnp.einsum("kgqp,pkd->qkgd", d_scores, keys_all, preferred_element_type=jnp.float32)
        * scaling
    )
    d_keys = (
        jnp.einsum("kgqp,qkgd->pkd", d_scores, queries, preferred_element_type=jnp.float32)
        * scaling
    )
    d_values = jnp.einsum(
        "kgqp,qkgd->pkd",
        probs_again.astype(jnp.bfloat16),
        d_attn,
        preferred_element_type=jnp.float32,
    )
    d_key_rows, d_value_rows = (
        lax.psum_scatter(
            d_keys.reshape(seq_rows, KV_HEADS * HEAD_DIM).astype(jnp.bfloat16),
            "col",
            scatter_dimension=0,
            tiled=True,
        ).astype(jnp.float32),
        lax.psum_scatter(
            d_values.reshape(seq_rows, KV_HEADS * HEAD_DIM).astype(jnp.bfloat16),
            "col",
            scatter_dimension=0,
            tiled=True,
        ).astype(jnp.float32),
    )
    d_query_rows = rotate(d_queries.reshape(rows_here, HEADS, HEAD_DIM), places, -1.0)
    d_key_rows = rotate(d_key_rows.reshape(rows_here, KV_HEADS, HEAD_DIM), places, -1.0)
    d_qkv = jnp.concatenate(
        [
            d_query_rows.reshape(rows_here, groups, q_cols),
            d_key_rows.reshape(rows_here, groups, kv_cols),
            d_value_rows.reshape(rows_here, groups, kv_cols),
        ],
        axis=2,
    )
    d_qkv = d_qkv.reshape(rows_here, groups * (q_cols + 2 * kv_cols)).astype(jnp.bfloat16)
    d_normed_one, qkv_grad = backward_project(d_qkv, qkv_block, normed_one_cols)
    d_tokens, attn_gain_part = norm_back(d_normed_one, unit_one, inverse_one, attn_gain)
    input_grad = d_tokens + d_middle
    gain_sums = lax.psum((attn_gain_part, ffn_gain_part), "col")
    summed = (
        lax.psum(qkv_grad.astype(jnp.bfloat16), "dp").astype(jnp.float32),
        lax.psum(o_grad.astype(jnp.bfloat16), "dp").astype(jnp.float32),
        lax.psum(gate_up_grad.astype(jnp.bfloat16), "dp").astype(jnp.float32),
        lax.psum(down_grad.astype(jnp.bfloat16), "dp").astype(jnp.float32),
        lax.psum(gain_sums[0].astype(jnp.bfloat16), "dp").astype(jnp.float32),
        lax.psum(gain_sums[1].astype(jnp.bfloat16), "dp").astype(jnp.float32),
    )
    qkv_total = summed[0]
    gate_up_total = summed[2]
    return (
        block_out,
        input_grad,
        summed[4],
        qkv_total[:, :q_cols],
        qkv_total[:, q_cols : q_cols + kv_cols],
        qkv_total[:, q_cols + kv_cols :],
        summed[1],
        summed[5],
        gate_up_total[:, :ff_cols],
        gate_up_total[:, ff_cols:],
        summed[3],
    )


def solution(mesh):
    return jax.shard_map(
        shards,
        mesh=mesh,
        in_specs=(
            P(("dp", "col"), None),
            P(("dp", "col")),
            P(),
            P("row", "col"),
            P("row", "col"),
            P("row", "col"),
            P("row", "col"),
            P(),
            P("row", "col"),
            P("row", "col"),
            P("row", "col"),
            P(("dp", "col"), None),
        ),
        out_specs=(
            P(("dp", "col"), None),
            P(("dp", "col"), None),
            P(),
            P("row", "col"),
            P("row", "col"),
            P("row", "col"),
            P("row", "col"),
            P(),
            P("row", "col"),
            P("row", "col"),
            P("row", "col"),
        ),
        check_vma=False,
    )
```

profile of v0, /device:TPU:0, one launch (start us, length us, event | category | flops | bytes accessed | tf_op | source)
XLA Modules:
  0.0 874.7 jit_solution(10202510273960042090)
XLA Ops:
  13.5 9.8 %all_gather.33 = bf16[1024,480]{0,1:T(8,128)(2,1)S(1)} all-gather(bf16[256,480]{0,1:T(8,128)(2,1)S(1)} %fusion.39), channel_id=1, replica_groups=mesh['dp'=16,'row'=2,'col'=4] {'col'}, dimensions={0}, use_global_device_ids=true | all-gather | bytes 1228800 | tf_op jit(solution)/shard_map/all_gather | solution.py:52
  26.4 3.6 all-to-all-start
  30.1 21.6 %all-gather = s32[4,1,256]{2,1,0:T(1,128)S(1)} all-gather(s32[1,1,256]{2,1,0:T(1,128)S(1)} %bitcast.195), channel_id=1, replica_groups=mesh['dp'=16,'row'=2,'col'=4] {'col'}, dimensions={0}, use_global_device_ids=true | all-gather | bytes 5120 | tf_op jit(solution)/shard_map/all_gather | solution.py:109
  52.4 46.1 %all-reduce.14 = bf16[256,1600]{0,1:T(8,128)(2,1)S(1)} all-reduce(f32[256,1600]{0,1:T(8,128)S(1)} %bitcast.149), channel_id=1, replica_groups=mesh['dp'=16,'row'=2,'col'=4] {'row'}, use_global_device_ids=true, to_apply=%region_1.0 | all-reduce | flops 409600 | bytes 2457600 | tf_op jit(solution)/shard_map/psum | solution.py:55
  98.9 6.9 all_gather.36
  105.8 8.0 all_gather.34
  113.8 6.7 fusion.50
  120.5 7.6 fusion.3
  128.1 7.1 fusion.23
  135.2 9.8 %all_gather.37 = bf16[1024,480]{0,1:T(8,128)(2,1)S(1)} all-gather(bf16[256,480]{0,1:T(8,128)(2,1)S(1)} %constant_dynamic-slice_fusion), channel_id=1, replica_groups=mesh['dp'=16,'row'=2,'col'=4] {'col'}, dimensions={0}, use_global_device_ids=true | all-gather | bytes 1228800 | tf_op jit(solution)/shard_map/all_gather | solution.py:52
  146.6 17.0 %all_to_all.146 = f32[4,256,240]{1,2,0:T(8,128)} all-to-all(f32[4,256,240]{1,2,0:T(8,128)S(1)} %bitcast.164), channel_id=1, replica_groups=mesh['dp'=16,'row'=2,'col'=4] {'col'}, dimensions={0} | all-to-all | bytes 1966080 | tf_op jit(solution)/shard_map/all_to_all | solution.py:54
  163.7 3.5 all-to-all-start.4
  169.1 7.9 all-to-all-done.4
  180.2 40.0 %all-reduce.9.cloned.1.call-done = f32[256,960]{0,1:T(8,128)} async-done(((f32[256,960]{0,1:T(8,128)}), f32[256,960]{0,1:T(8,128)}) %all-reduce.9.cloned.1.call-update) | async-done | bytes 983056 | tf_op jit(solution)/shard_map/psum | solution.py:55
  224.1 8.9 %all_gather.38 = bf16[1024,480]{0,1:T(8,128)(2,1)S(1)} all-gather(bf16[256,480]{0,1:T(8,128)(2,1)S(1)} %fusion.38), channel_id=1, replica_groups=mesh['dp'=16,'row'=2,'col'=4] {'col'}, dimensions={0}, use_global_device_ids=true | all-gather | bytes 1228800 | tf_op jit(solution)/shard_map/all_gather | solution.py:52
  233.0 5.5 fusion.52
  238.6 5.9 copy.72
  244.5 5.1 all-to-all-start.2
  250.3 72.7 %all-to-all-done.2 = f32[4,256,1280]{1,2,0:T(8,128)} async-done(((f32[4,256,1280]{1,2,0:T(8,128)}), f32[4,256,1280]{1,2,0:T(8,128)}, u32[]{:S(2)}, u32[]{:S(2)}) %all-to-all-start.2) | async-done | bytes 5242912 | tf_op jit(solution)/shard_map/all_to_all | solution.py:54
  323.0 125.8 %all-reduce.15 = bf16[256,5120]{0,1:T(8,128)(2,1)S(1)} all-reduce(f32[256,5120]{0,1:T(8,128)} %bitcast.24), channel_id=1, replica_groups=mesh['dp'=16,'row'=2,'col'=4] {'row'}, use_global_device_ids=true, to_apply=%region_7.8 | all-reduce | flops 1310720 | bytes 7864320 | tf_op jit(solution)/shard_map/psum | solution.py:55
  448.9 2.8 fusion.47
  451.7 3.2 copy.95
  457.0 6.2 fusion.11
  463.7 33.8 %all_to_all.147 = bf16[256,4,1280]{2,0,1:T(8,128)(2,1)S(1)} all-to-all(bf16[256,4,1280]{2,0,1:T(8,128)(2,1)S(1)} %pad_maximum_fusion), channel_id=1, replica_groups=mesh['dp'=16,'row'=2,'col'=4] {'col'}, dimensions={1} | all-to-all | bytes 5242880 | tf_op jit(solution)/shard_map/all_to_all | solution.py:60
  499.0 3.8 convolution_convert_fusion.5
  502.8 19.7 %reduce-scatter.9.cloned.1.call-done = bf16[256,480]{0,1:T(8,128)(2,1)} async-done(((bf16[1024,480]{0,1:T(8,128)(2,1)}), bf16[256,480]{0,1:T(8,128)(2,1)}) %reduce-scatter.9.cloned.1.call-update) | async-done | bytes 245776 | tf_op jit(solution)/shard_map/reduce_scatter | solution.py:64
  522.6 10.7 %all_gather.41 = bf16[256,960]{0,1:T(8,128)(2,1)S(1)} all-gather(bf16[256,480]{0,1:T(8,128)(2,1)} %reduce-scatter.9.cloned.1.call-done), channel_id=1, replica_groups=mesh['dp'=16,'row'=2,'col'=4] {'row'}, dimensions={1}, use_global_device_ids=true | all-gather | bytes 737280 | tf_op jit(solution)/shard_map/all_gather | solution.py:72
  535.7 11.0 %all_to_all.148 = bf16[256,4,240]{0,2,1:T(8,128)(2,1)S(1)} all-to-all(bf16[256,4,240]{0,2,1:T(8,128)(2,1)S(1)} %bitcast.180), channel_id=1, replica_groups=mesh['dp'=16,'row'=2,'col'=4] {'col'}, dimensions={1} | all-to-all | bytes 983040 | tf_op jit(solution)/shard_map/all_to_all | solution.py:60
  549.0 20.0 %reduce-scatter.11.cloned.1.call-done = bf16[256,480]{0,1:T(8,128)(2,1)} async-done(((bf16[1024,480]{0,1:T(8,128)(2,1)}), bf16[256,480]{0,1:T(8,128)(2,1)}) %reduce-scatter.11.cloned.1.call-update) | async-done | bytes 245776 | tf_op jit(solution)/shard_map/reduce_scatter | solution.py:64
  569.0 10.9 %all_gather.42 = bf16[256,960]{0,1:T(8,128)(2,1)S(1)} all-gather(bf16[256,480]{0,1:T(8,128)(2,1)} %reduce-scatter.11.cloned.1.call-done), channel_id=1, replica_groups=mesh['dp'=16,'row'=2,'col'=4] {'row'}, dimensions={1}, use_global_device_ids=true | all-gather | bytes 737280 | tf_op jit(solution)/shard_map/all_gather | solution.py:72
  579.9 12.8 %fusion = (f32[5,3,256]{2,1,0:T(4,128)S(1)}, f32[5,1024,256,3]{2,1,3,0:T(8,128)}) fusion(f32[5,3,256,1024]{2,3,1,0:T(8,128)} %get-tuple-element.90, f32[5,3,256]{2,1,0:T(4,128)S(1)} %log_add_fusion, bf16[1024,5,64,1]{0,2,3,1:T(8,128)(2,1)S(1)} %bitcast.158, bf16[256,5,3,64]{0,3,2,1:T(8,128)(2,1)S(1)} %bitcast.145), kind=kOutput, calls=%fused_computation.2 | convolution fusion | flops 515109120 | bytes 32634880 | tf_op jit(solution)/shard_map/qkgd,pkd->kgqp/dot_general | solution.py:181
  595.4 7.7 fusion.2
  603.1 3.4 fusion.18
  606.6 8.9 %fusion.19 = bf16[5,64,1024]{2,1,0:T(8,128)(2,1)} fusion(bf16[256,5,3,64]{0,3,2,1:T(8,128)(2,1)S(1)} %bitcast.146, f32[5,3,256,1024]{2,3,1,0:T(8,128)} %get-tuple-element.90, f32[5,3,256]{2,1,0:T(4,128)S(1)} %log_add_fusion), kind=kOutput, calls=%fused_computation.38 | convolution fusion | flops 511508480 | bytes 16890880 | tf_op jit(solution)/shard_map/kgqp,qkgd->pkd/dot_general | solution.py:192
  615.5 2.8 fusion.22
  618.5 4.8 convolution_multiply_fusion
  623.4 2.7 reduce-scatter.13.cloned.1.call-done
  627.1 21.7 %reduce-scatter.15.cloned.1.call-done = bf16[256,320]{0,1:T(8,128)(2,1)} async-done(((bf16[1024,320]{0,1:T(8,128)(2,1)}), bf16[256,320]{0,1:T(8,128)(2,1)}) %reduce-scatter.15.cloned.1.call-update) | async-done | bytes 163856 | tf_op jit(solution)/shard_map/reduce_scatter | solution.py:205
  649.9 14.4 %all_to_all.149 = bf16[256,4,400]{0,2,1:T(8,128)(2,1)S(1)} all-to-all(bf16[256,4,400]{0,2,1:T(8,128)(2,1)S(1)} %pad_maximum_fusion.1), channel_id=1, replica_groups=mesh['dp'=16,'row'=2,'col'=4] {'col'}, dimensions={1} | all-to-all | bytes 1638400 | tf_op jit(solution)/shard_map/all_to_all | solution.py:60
  666.2 19.0 %all-gather.4.cloned.1.call-done = bf16[1024,1280]{1,0:T(8,128)(2,1)} async-done(((bf16[256,1280]{1,0:T(8,128)(2,1)}), bf16[1024,1280]{1,0:T(8,128)(2,1)}) %all-gather.4.cloned.1.call-update) | async-done | bytes 2621456 | tf_op jit(solution)/shard_map/all_gather | solution.py:52
  685.2 2.6 fusion.53
  687.9 22.0 %all_to_all.150 = f32[4,256,240]{1,2,0:T(8,128)} all-to-all(f32[4,256,240]{1,2,0:T(8,128)S(1)} %bitcast.165), channel_id=1, replica_groups=mesh['dp'=16,'row'=2,'col'=4] {'col'}, dimensions={0} | all-to-all | bytes 1966080 | tf_op jit(solution)/shard_map/all_to_all | solution.py:54
  710.0 4.7 convolution_convert_fusion.1
  719.0 16.0 %all_gather.43 = bf16[256,960]{0,1:T(8,128)(2,1)S(1)} all-gather(bf16[256,480]{0,1:T(8,128)(2,1)} %reduce-scatter.17.cloned.1.call-done), channel_id=1, replica_groups=mesh['dp'=16,'row'=2,'col'=4] {'row'}, dimensions={1}, use_global_device_ids=true | all-gather | bytes 737280 | tf_op jit(solution)/shard_map/all_gather | solution.py:72
  736.3 5.9 all-reduce
  742.1 40.6 %all-reduce.1 = (bf16[960]{0:T(1024)(128)(2,1)S(1)}, bf16[960]{0:T(1024)(128)(2,1)S(1)}) all-reduce(bf16[960]{0:T(1024)(128)(2,1)S(1)} %get-tuple-element.59, bf16[960]{0:T(1024)(128)(2,1)S(1)} %get-tuple-element.60), channel_id=1, replica_groups=mesh['dp'=16,'row'=2,'col'=4] {'dp'}, use_global_device_ids=true, to_apply=%region_20.21 | all-reduce | flops 1920 | bytes 7680 | tf_op jit(solution)/shard_map/psum | solution.py:232
  783.9 3.6 fusion.31
  787.5 72.7 %all-reduce.13.cloned.1.call-done = (bf16[480,400]{0,1:T(8,128)(2,1)}, bf16[480,1280]{1,0:T(8,128)(2,1)}, bf16[480,240]{1,0:T(8,128)(2,1)}, bf16[1280,240]{0,1:T(8,128)(2,1)}) async-done(((bf16[480,400]{0,1:T(8,128)(2,1)}, bf16[480,1280]{1,0:T(8,128)(2,1)}, bf16[480,240]{1,0:T(8,128)(2,1)}, bf16[1280,240]{0,1:T(8,128)(2,1)}), (bf16[480,400]{0,1:T(8,128)(2,1)}, bf16[480,1280]{1,0:T(8,128)(2,1)}, ...) | async-done | bytes 2457616 | tf_op jit(solution)/shard_map/psum | solution.py:228
  (202 shorter events, 50.9 us)
Async XLA Ops:
  8.0 169.8 %copy-start = (bf16[1280,240]{0,1:T(8,128)(2,1)S(1)}, bf16[1280,240]{0,1:T(8,128)(2,1)}, u32[]{:S(2)}) copy-start(bf16[1280,240]{0,1:T(8,128)(2,1)} %param.22) | copy-start | bytes 1843204
  8.0 16.3 %copy-start.37 = (bf16[480,240]{1,0:T(8,128)(2,1)S(1)}, bf16[480,240]{1,0:T(8,128)(2,1)}, u32[]{:S(2)}) copy-start(bf16[480,240]{1,0:T(8,128)(2,1)} %param.15) | copy-start | bytes 691204
  9.3 15.7 %copy-start.45 = (f32[256]{0:T(256)}, f32[256]{0:T(256)S(1)}, u32[]{:S(2)}) copy-start(f32[256]{0:T(256)S(1)} %add_rsqrt_fusion.1) | copy-start | bytes 3076
  10.4 14.7 %copy-start.33 = (bf16[480,80]{1,0:T(8,128)(2,1)}, bf16[480,80]{1,0:T(8,128)(2,1)S(1)}, u32[]{:S(2)}) copy-start(bf16[480,80]{1,0:T(8,128)(2,1)S(1)} %copy.67) | copy-start | bytes 230404
  11.5 13.6 %copy-start.35 = (bf16[480,80]{1,0:T(8,128)(2,1)}, bf16[480,80]{1,0:T(8,128)(2,1)S(1)}, u32[]{:S(2)}) copy-start(bf16[480,80]{1,0:T(8,128)(2,1)S(1)} %copy.68) | copy-start | bytes 230404
  26.4 25.9 %all-to-all-start = ((f32[4,256,400]{1,2,0:T(8,128)}), f32[4,256,400]{1,2,0:T(8,128)S(1)}, u32[]{:S(2)}, u32[]{:S(2)}) async-start(f32[4,256,400]{1,2,0:T(8,128)} %bitcast.150), calls=%async_computation | async-start | bytes 3276800 | tf_op jit(solution)/shard_map/all_to_all | solution.py:54
  30.0 190.2 %all-reduce.9.cloned.1.call-start = ((), (), s32[]{:S(2)}) async-start(), calls=%async_computation.14 | async-start | bytes 1966080 | tf_op jit(solution)/shard_map/psum | solution.py:55
  98.8 21.6 %copy-start.22 = (bf16[256,15,32]{0,2,1:T(8,128)(2,1)}, bf16[256,15,32]{0,2,1:T(8,128)(2,1)S(1)}, u32[]{:S(2)}) copy-start(bf16[256,15,32]{0,2,1:T(8,128)(2,1)S(1)} %get-tuple-element.76) | copy-start | bytes 737284
  98.9 21.6 %copy-start.24 = (bf16[256,15,32]{0,2,1:T(8,128)(2,1)}, bf16[256,15,32]{0,2,1:T(8,128)(2,1)S(1)}, u32[]{:S(2)}) copy-start(bf16[256,15,32]{0,2,1:T(8,128)(2,1)S(1)} %get-tuple-element.77) | copy-start | bytes 737284
  105.8 14.7 %copy-start.9 = (bf16[1024,320]{0,1:T(8,128)(2,1)}, bf16[1024,320]{0,1:T(8,128)(2,1)S(1)}, u32[]{:S(2)}) copy-start(bf16[1024,320]{0,1:T(8,128)(2,1)S(1)} %all_gather.36) | copy-start | bytes 1966084
  113.7 14.4 %copy-start.14 = (bf16[1024,320]{0,1:T(8,128)(2,1)}, bf16[1024,320]{0,1:T(8,128)(2,1)S(1)}, u32[]{:S(2)}) copy-start(bf16[1024,320]{0,1:T(8,128)(2,1)S(1)} %all_gather.34) | copy-start | bytes 1966084
  120.5 7.6 copy-start.40
  128.1 7.1 copy-start.41
  128.1 17.9 %copy-start.27 = (bf16[480,240]{1,0:T(8,128)(2,1)S(1)}, bf16[480,240]{1,0:T(8,128)(2,1)}, u32[]{:S(2)}) copy-start(bf16[480,240]{1,0:T(8,128)(2,1)} %param.18) | copy-start | bytes 691204
  146.5 20.7 %copy-start.42 = (f32[960]{0:T(1024)S(1)}, f32[960]{0:T(1024)}, u32[]{:S(2)}) copy-start(f32[960]{0:T(1024)} %param.19) | copy-start | bytes 11524
  146.5 20.8 %copy-start.31 = (bf16[480,640]{1,0:T(8,128)(2,1)S(1)}, bf16[480,640]{1,0:T(8,128)(2,1)}, u32[]{:S(2)}) copy-start(bf16[480,640]{1,0:T(8,128)(2,1)} %param.20) | copy-start | bytes 1843204
  146.6 21.6 %copy-start.32 = (bf16[480,640]{1,0:T(8,128)(2,1)S(1)}, bf16[480,640]{1,0:T(8,128)(2,1)}, u32[]{:S(2)}) copy-start(bf16[480,640]{1,0:T(8,128)(2,1)} %param.21) | copy-start | bytes 1843204
  163.7 13.3 %all-to-all-start.4 = ((bf16[256,4,240]{0,2,1:T(8,128)(2,1)}), bf16[256,4,240]{0,2,1:T(8,128)(2,1)S(1)}, u32[]{:S(2)}, u32[]{:S(2)}) async-start(bf16[256,4,240]{0,2,1:T(8,128)(2,1)} %bitcast.33), calls=%async_computation.4 | async-start | bytes 983040 | tf_op jit(solution)/shard_map/all_to_all | solution.py:60
  167.2 82.4 %reduce-scatter.7.cloned.1.call-start = ((), (), s32[]{:S(2)}) async-start(), calls=%async_computation.17 | async-start | bytes 3276800 | tf_op jit(solution)/shard_map/reduce_scatter | solution.py:64
  180.2 40.0 %copy-start.4 = (bf16[256,960]{0,1:T(8,128)(2,1)S(1)}, bf16[256,960]{0,1:T(8,128)(2,1)}, u32[]{:S(2)}) copy-start(bf16[256,960]{0,1:T(8,128)(2,1)} %param.12) | copy-start | bytes 1474564
  244.5 78.6 %all-to-all-start.2 = ((f32[4,256,1280]{1,2,0:T(8,128)}), f32[4,256,1280]{1,2,0:T(8,128)}, u32[]{:S(2)}, u32[]{:S(2)}) async-start(f32[4,256,1280]{1,2,0:T(8,128)} %copy.72), calls=%async_computation.2 | async-start | bytes 10485760 | tf_op jit(solution)/shard_map/all_to_all | solution.py:54
  249.5 207.5 %all-gather.6.cloned.1.call-start = ((), (), s32[]{:S(2)}) async-start(), calls=%async_computation.18 | async-start | bytes 1966080 | tf_op jit(solution)/shard_map/all_gather | solution.py:72
  250.3 272.3 %reduce-scatter.9.cloned.1.call-start = ((), (), s32[]{:S(2)}) async-start(), calls=%async_computation.19 | async-start | bytes 1228800 | tf_op jit(solution)/shard_map/reduce_scatter | solution.py:64
  499.0 34.3 %copy-start.3 = (f32[256,960]{0,1:T(8,128)S(1)}, f32[256,960]{0,1:T(8,128)}, u32[]{:S(2)}) copy-start(f32[256,960]{0,1:T(8,128)} %copy-done.2) | copy-start | bytes 2949124
  502.8 66.2 %reduce-scatter.11.cloned.1.call-start = ((), (), s32[]{:S(2)}) async-start(), calls=%async_computation.20 | async-start | bytes 1228800 | tf_op jit(solution)/shard_map/reduce_scatter | solution.py:64
  533.3 13.5 %copy-start.8 = (bf16[256,960]{0,1:T(8,128)(2,1)}, bf16[256,960]{0,1:T(8,128)(2,1)S(1)}, u32[]{:S(2)}) copy-start(bf16[256,960]{0,1:T(8,128)(2,1)S(1)} %all_gather.41) | copy-start | bytes 1474564
  535.7 44.2 %copy-start.15 = (bf16[1024,320]{0,1:T(8,128)(2,1)S(1)}, bf16[1024,320]{0,1:T(8,128)(2,1)}, u32[]{:S(2)}) copy-start(bf16[1024,320]{0,1:T(8,128)(2,1)} %copy-done.14) | copy-start | bytes 1966084
  548.2 77.9 %reduce-scatter.13.cloned.1.call-start = ((), (), s32[]{:S(2)}) async-start(), calls=%async_computation.21 | async-start | bytes 819200 | tf_op jit(solution)/shard_map/reduce_scatter | solution.py:199
  579.9 12.8 %slice-start = ((s8[15728640]{0:T(1024)(128)(4,1)}), s8[4194304]{0:T(1024)(128)(4,1)S(1)}, s32[]{:S(2)}) async-start(s8[15728640]{0:T(1024)(128)(4,1)} %bitcast.139), calls=%async_computation.25 | async-start | bytes 8388608
  579.9 12.8 %slice-start.1 = ((s8[15728640]{0:T(1024)(128)(4,1)}), s8[4194304]{0:T(1024)(128)(4,1)S(1)}, s32[]{:S(2)}) async-start(s8[15728640]{0:T(1024)(128)(4,1)} %bitcast.139), calls=%async_computation.26 | async-start | bytes 8388608
  579.9 14.6 %slice-start.2 = ((s8[15728640]{0:T(1024)(128)(4,1)}), s8[4194304]{0:T(1024)(128)(4,1)S(1)}, s32[]{:S(2)}) async-start(s8[15728640]{0:T(1024)(128)(4,1)} %bitcast.139), calls=%async_computation.27 | async-start | bytes 8388608
  579.9 15.5 %slice-start.3 = ((s8[15728640]{0:T(1024)(128)(4,1)}), s8[3145728]{0:T(1024)(128)(4,1)S(1)}, s32[]{:S(2)}) async-start(s8[15728640]{0:T(1024)(128)(4,1)} %bitcast.139), calls=%async_computation.28 | async-start | bytes 6291456
  595.4 7.7 copy-start.23
  595.4 7.7 copy-start.25
  606.5 42.3 %reduce-scatter.15.cloned.1.call-start = ((), (), s32[]{:S(2)}) async-start(), calls=%async_computation.22 | async-start | bytes 819200 | tf_op jit(solution)/shard_map/reduce_scatter | solution.py:205
  615.5 69.7 %all-gather.4.cloned.1.call-start = ((), (), s32[]{:S(2)}) async-start(), calls=%async_computation.15 | async-start | bytes 3276800 | tf_op jit(solution)/shard_map/all_gather | solution.py:52
  618.4 100.5 %reduce-scatter.17.cloned.1.call-start = ((), (), s32[]{:S(2)}) async-start(), calls=%async_computation.23 | async-start | bytes 1228800 | tf_op jit(solution)/shard_map/reduce_scatter | solution.py:64
  627.1 37.3 %copy-start.34 = (bf16[480,80]{1,0:T(8,128)(2,1)S(1)}, bf16[480,80]{1,0:T(8,128)(2,1)}, u32[]{:S(2)}) copy-start(bf16[480,80]{1,0:T(8,128)(2,1)} %copy-done.33) | copy-start | bytes 230404
  627.1 37.3 %copy-start.36 = (bf16[480,80]{1,0:T(8,128)(2,1)S(1)}, bf16[480,80]{1,0:T(8,128)(2,1)}, u32[]{:S(2)}) copy-start(bf16[480,80]{1,0:T(8,128)(2,1)} %copy-done.35) | copy-start | bytes 230404
  627.1 37.3 %copy-start.38 = (bf16[480,240]{1,0:T(8,128)(2,1)S(1)}, bf16[480,240]{1,0:T(8,128)(2,1)}, u32[]{:S(2)}) copy-start(bf16[480,240]{1,0:T(8,128)(2,1)} %param.15) | copy-start | bytes 691204
  666.1 117.8 %all-reduce.11.cloned.1.call-start = ((), (), s32[]{:S(2)}) async-start(), calls=%async_computation.16 | async-start | bytes 1966080 | tf_op jit(solution)/shard_map/psum | solution.py:55
  709.9 150.3 %all-reduce.13.cloned.1.call-start = ((), (), s32[]{:S(2)}) async-start(), calls=%async_computation.24 | async-start | bytes 4997120 | tf_op jit(solution)/shard_map/psum | solution.py:228
  717.5 18.2 %copy-start.5 = (bf16[256,960]{0,1:T(8,128)(2,1)S(1)}, bf16[256,960]{0,1:T(8,128)(2,1)}, u32[]{:S(2)}) copy-start(bf16[256,960]{0,1:T(8,128)(2,1)} %param.12) | copy-start | bytes 1474564
  717.5 18.2 %copy-start.43 = (f32[960]{0:T(1024)S(1)}, f32[960]{0:T(1024)}, u32[]{:S(2)}) copy-start(f32[960]{0:T(1024)} %param.14) | copy-start | bytes 11524
  717.5 18.2 %copy-start.46 = (f32[256]{0:T(256)S(1)}, f32[256]{0:T(256)}, u32[]{:S(2)}) copy-start(f32[256]{0:T(256)} %copy-done.45) | copy-start | bytes 3076
  718.9 17.4 %copy-start.44 = (f32[960]{0:T(1024)S(1)}, f32[960]{0:T(1024)}, u32[]{:S(2)}) copy-start(f32[960]{0:T(1024)} %get-tuple-element.55) | copy-start | bytes 11524
  718.9 65.0 %copy-start.7 = (f32[256,960]{0,1:T(8,128)S(1)}, f32[256,960]{0,1:T(8,128)}, u32[]{:S(2)}) copy-start(f32[256,960]{0,1:T(8,128)} %all-reduce.9.cloned.1.call-done) | copy-start | bytes 2949124
  718.9 65.0 %copy-start.48 = (f32[256]{0:T(256)S(1)}, f32[256]{0:T(256)}, u32[]{:S(2)}) copy-start(f32[256]{0:T(256)} %copy-done.47) | copy-start | bytes 3076
  (21 other events, 63.1 us)
Sparse Core Ops, SparseCore 0:
  163.8 56.3 all-reduce.8
  252.1 43.2 all-gather.5
  710.0 52.9 all-reduce.10
  767.8 92.3 all-reduce.12
Sparse Core Ops, SparseCore 1:
  180.3 43.7 reduce-scatter.6
  502.9 19.6 reduce-scatter.8
  548.2 20.7 reduce-scatter.10
  606.6 19.4 reduce-scatter.12
  629.2 19.6 reduce-scatter.14
  651.2 33.9 all-gather.3
  688.2 24.9 reduce-scatter.16
where the time goes:
time: 877 us; the launch traced here: 875 us
  blocking collectives  419 us (48%)
  waiting for transfers between devices  277 us (32%)
  matrix products  71 us (8%)
  other arithmetic  43.4 us (5%)
  local copies, waits for them, and re-layouts  34.9 us (4%)
  between operations  16.1 us (2%)
  starting transfers between devices  12.6 us (1%)
    psum x2, blocking collectives, forward_project(): result = lax.psum(arrived, 'row')  172 us
    psum x1, waiting for transfers between devices, shards(): lax.psum(qkv_grad.astype(jnp.bfloat16), 'dp').astype(jnp.float32)  72.7 us
    all_to_all x2, waiting for transfers between devices, forward_project(): lax.all_to_all(partial_out, 'col', split_axis=0, concat_axis=1, tiled=True)  72.7 us
    all_to_all x3, blocking collectives, backward_project(): lax.all_to_all(gradient, 'col', split_axis=1, concat_axis=0, tiled=True)  59.2 us
    psum x1, blocking collectives, shards(): lax.psum(gain_sums[0].astype(jnp.bfloat16), 'dp').astype(jnp.float32)  40.6 us
    psum x2, waiting for transfers between devices, forward_project(): result = lax.psum(arrived, 'row')  40 us
    reduce_scatter x4, waiting for transfers between devices, backward_project(): lax.psum_scatter(lax.dot_general(grad_cols, weight_block, (((1,), (1,)),...  39.8 us
    all_to_all x2, blocking collectives, forward_project(): lax.all_to_all(partial_out, 'col', split_axis=0, concat_axis=1, tiled=True)  39.1 us
  transfers between devices with their start and end apart: 14, of which 9 were waited for; matrix products, arithmetic and copies ran while one was open for 7% of the time, Pallas kernels for 0%

commit v1 on v0

v1 whole, which is shorter than its diff:
```python
import jax
import jax.numpy as jnp
import numpy as np
from jax import lax
from jax.experimental import pallas as pl
from jax.experimental.pallas import tpu as pltpu
from jax.sharding import PartitionSpec as P

HEADS = 15
KV_HEADS = 5
HEAD_DIM = 64
SHARE = HEADS // KV_HEADS
D = 960
HALF = 480
QD = 960
KVD = 320
UNITS = 640
OWN = 128
KEYS = 1024
SCALING = HEAD_DIM ** (-0.5)
MESH = pl.DeviceIdType.MESH
F32 = jnp.float32
BF16 = jnp.bfloat16
SLOTS = 288
CHUNKS = 15

norm_eps = 1e-05
rope_base = 100000.0


def dot(a, b):
    return jnp.dot(a, b, preferred_element_type=F32)


def dot_nt(a, b):
    return lax.dot_general(a, b, (((1,), (1,)), ((), ())), preferred_element_type=F32)


def dot_tn(a, b):
    return lax.dot_general(a, b, (((0,), (0,)), ((), ())), preferred_element_type=F32)


def heads_of(x, group):
    first = group * SHARE
    return jnp.concatenate(
        [x[:, (first + j) * HEAD_DIM : (first + j + 1) * HEAD_DIM] for j in range(SHARE)], axis=0
    )


def rows_of(index, count):
    return pl.ds(pl.multiple_of(index * count, count), count)


class Place:
    def __init__(self, send_sem, recv_sem):
        col = lax.axis_index("col")
        self.dp, self.row = lax.axis_index("dp"), lax.axis_index("row")
        self.ranks = lax.axis_size("dp")
        self.z, self.x = self.dp // 4, self.dp % 4
        self.low, self.s = col // 2, col % 2
        self.y = self.row * 2 + self.low
        self.up, self.down, self.far = (self.y + 1) % 4, (self.y + 3) % 4, (self.y + 2) % 4
        self.send_sem, self.recv_sem, self.used = send_sem, recv_sem, 0
        self.open = []

    def device(self, y, s):
        return (self.dp, y // 2, (y % 2) * 2 + s)

    def rank(self, z, x):
        return (z * 4 + x, self.row, self.low * 2 + self.s)

    def peer(self, k):
        return ((self.dp + k) % self.ranks, self.row, self.low * 2 + self.s)

    def slots(self, count):
        first = self.used
        self.used += count
        assert self.used <= SLOTS
        return first

    def wire(self, src, dst, other, slot, recv_slot=None):
        return pltpu.make_async_remote_copy(
            src_ref=src,
            dst_ref=dst,
            send_sem=self.send_sem.at[slot],
            recv_sem=self.recv_sem.at[slot if recv_slot is None else recv_slot],
            device_id=other,
            device_id_type=MESH,
        )

    def send(self, src, dst, other):
        copy = self.wire(src, dst, other, self.slots(1))
        copy.start()
        self.open.append(copy)
        return copy

    def others(self):
        others = [self.peer(k) for k in range(1, self.ranks)]
        others += [self.device(self.y, 1 - self.s)]
        for y in (self.up, self.down, self.far):
            others += [self.device(y, self.s), self.device(y, 1 - self.s)]
        return others

    def greet(self):
        barrier = pltpu.get_barrier_semaphore()
        for other in self.others():
            pl.semaphore_signal(barrier, inc=1, device_id=other, device_id_type=MESH)

    def meet(self):
        pl.semaphore_wait(pltpu.get_barrier_semaphore(), len(self.others()))


class Gather:
    def __init__(self, at, buf, rows, split, index=None):
        self.at, self.buf = at, buf
        self.both = index is not None
        if index is None:
            self.mine, self.low, self.high, self.opposite = 0, 1, 2, 3
            self.to_up, self.to_down, self.on_up, self.on_down = 1, 2, 3, 3
        else:
            self.mine, self.low = index(at.y, at.s), index(at.down, at.s)
            self.high, self.opposite = index(at.up, at.s), index(at.far, at.s)
            self.to_up, self.to_down = self.mine, self.mine
            self.on_up, self.on_down = self.low, self.high
        self.first, self.second = pl.ds(0, split), pl.ds(split, rows - split)
        self.up_device, self.down_device = at.device(at.up, at.s), at.device(at.down, at.s)
        self.mate = at.device(at.y, 1 - at.s)
        self.from_mate = []

    def ship(self, index, part, to_index, other):
        return self.at.send(self.buf.at[index, part], self.buf.at[to_index, part], other)

    def to_mate(self, index):
        if self.both:
            self.from_mate.append(self.at.send(self.buf.at[index], self.buf.at[index], self.mate))

    def start(self):
        self.up_first = self.ship(self.mine, self.first, self.to_up, self.up_device)
        self.down_second = self.ship(self.mine, self.second, self.to_down, self.down_device)
        self.up_second = self.ship(self.mine, self.second, self.to_up, self.up_device)
        self.down_first = self.ship(self.mine, self.first, self.to_down, self.down_device)
        self.to_mate(self.mine)

    def relay(self):
        self.up_first.wait_recv()
        self.up_far = self.ship(self.low, self.first, self.on_up, self.up_device)
        self.down_second.wait_recv()
        self.down_far = self.ship(self.high, self.second, self.on_down, self.down_device)

    def near(self):
        self.up_second.wait_recv()
        self.to_mate(self.low)
        self.down_first.wait_recv()
        self.to_mate(self.high)

    def finish(self):
        self.up_far.wait_recv()
        self.down_far.wait_recv()
        self.to_mate(self.opposite)
        for copy in self.from_mate:
            copy.wait_recv()


class Reduce:
    def __init__(self, at, blocks, early, sums, landed):
        self.at, self.blocks = at, blocks
        self.early, self.sums, self.landed = early, sums, landed
        self.up_device, self.down_device = at.device(at.up, at.s), at.device(at.down, at.s)

    def start_far(self):
        at, far = self.at, self.blocks.at[3]
        self.first = at.send(far.at[0], self.early.at[0], self.down_device)
        self.second = at.send(far.at[1], self.early.at[1], self.up_device)

    def start_near(self):
        at = self.at
        self.third = at.send(self.blocks.at[1, 1], self.landed.at[0, 1], self.down_device)
        self.fourth = at.send(self.blocks.at[2, 0], self.landed.at[1, 0], self.up_device)

    def middle(self):
        at, blocks, early, sums = self.at, self.blocks, self.early, self.sums
        self.first.wait_recv()
        sums[0] = (blocks[1, 0].astype(F32) + early[0].astype(F32)).astype(BF16)
        self.fifth = at.send(sums.at[0], self.landed.at[0, 0], self.down_device)
        self.second.wait_recv()
        sums[1] = (blocks[2, 1].astype(F32) + early[1].astype(F32)).astype(BF16)
        self.sixth = at.send(sums.at[1], self.landed.at[1, 1], self.up_device)

    def finish(self):
        for copy in (self.third, self.fourth, self.fifth, self.sixth):
            copy.wait_recv()
        total = (
            self.blocks[0].astype(F32) + self.landed[0].astype(F32) + self.landed[1].astype(F32)
        )
        return total.reshape(total.shape[0] * total.shape[1], total.shape[2])


class RankSum:
    def __init__(self, at, halves, mate, kept, parts, total, out):
        self.at, self.halves, self.mate, self.kept = at, halves, mate, kept
        self.parts, self.total, self.out = parts, total, out

    def start(self):
        at = self.at
        self.swap = at.send(self.halves.at[1 - at.s], self.mate, at.device(at.y, 1 - at.s))

    def join(self):
        at = self.at
        self.swap.wait_recv()

        def add(i, carry):
            rows = rows_of(i, 32)
            self.kept[rows] = (
                self.halves[at.s, rows].astype(F32) + self.mate[rows].astype(F32)
            ).astype(BF16)
            return carry

        lax.fori_loop(0, 16, add, 0)

    def scatter(self):
        at = self.at
        self.join()
        self.copies = [
            at.send(self.kept.at[rows_of((at.dp + k) % at.ranks, 32)], self.parts.at[k - 1], at.peer(k))
            for k in range(1, at.ranks)
        ]

    def reduce(self):
        at = self.at
        acc = self.kept[rows_of(at.dp, 32)].astype(F32)
        for k, copy in enumerate(self.copies):
            copy.wait_recv()
            acc = acc + self.parts[k].astype(F32)
        self.total[...] = acc.astype(BF16)

    def gather(self):
        at = self.at
        own = self.out.at[rows_of(at.dp, 32)]
        self.back = [at.send(own, own, at.peer(k)) for k in range(1, at.ranks)]

    def finish(self):
        for copy in self.back:
            copy.wait_recv()


class Spread:
    def __init__(self, at, buf, guard=None):
        self.at, self.buf, self.guard = at, buf, guard
        self.slot = at.slots(18)

    def guarded(self, act):
        if self.guard is None:
            act()
        else:
            pl.when(self.guard)(act)

    def along(self, half, second, step):
        at = self.at
        if (half == 0) != second:
            return at.rank((at.z + step) % 4, at.x)
        return at.rank(at.z, (at.x + step) % 4)

    def first_copy(self, half, n):
        own = self.buf.at[self.at.z, self.at.x, half]
        return self.at.wire(own, own, self.along(half, False, (1, 3, 2)[n]), self.slot + half * 9 + n)

    def block(self, half, part, back):
        at, pair = self.at, pl.ds(2 * part, 2)
        if half == 0:
            return self.buf.at[pair, (at.x + 4 - back) % 4, half]
        return self.buf.at[(at.z + 4 - back) % 4, pair, half]

    def second_copy(self, half, n):
        step, part = ((1, 0), (3, 1), (1, 1), (3, 0))[n]
        src = self.block(half, part, 0)
        return self.at.wire(src, src, self.along(half, True, step), self.slot + half * 9 + 3 + n)

    def third_copy(self, half, n):
        step, part = ((1, 0), (3, 1))[n]
        src = self.block(half, part, step)
        return self.at.wire(src, src, self.along(half, True, step), self.slot + half * 9 + 7 + n)

    def first(self):
        def act():
            for half in range(2):
                for n in range(3):
                    self.first_copy(half, n).start()

        self.guarded(act)

    def second(self):
        def act():
            for half in range(2):
                for n in range(3):
                    self.first_copy(half, n).wait_recv()
                for n in range(4):
                    self.second_copy(half, n).start()

        self.guarded(act)

    def third(self):
        def act():
            for n in range(2):
                for half in range(2):
                    self.second_copy(half, n).wait_recv()
                    self.third_copy(half, n).start()

        self.guarded(act)

    def finish(self):
        def act():
            for half in range(2):
                for n in range(2, 4):
                    self.second_copy(half, n).wait_recv()
                for n in range(2):
                    self.third_copy(half, n).wait_recv()

        self.guarded(act)

    def drain(self):
        def act():
            for half in range(2):
                for n in range(3):
                    self.first_copy(half, n).wait_send()
                for n in range(4):
                    self.second_copy(half, n).wait_send()
                for n in range(2):
                    self.third_copy(half, n).wait_send()

        self.guarded(act)


class Collect:
    def __init__(self, at, kept, early, sums, landed, four, parts, total):
        self.at, self.kept, self.early, self.sums = at, kept, early, sums
        self.landed, self.four, self.parts, self.total = landed, four, parts, total

    def along(self, half, second, step):
        at = self.at
        if (half == 1) != second:
            return at.rank((at.z + step) % 4, at.x)
        return at.rank(at.z, (at.x + step) % 4)

    def block(self, half, step, part):
        at = self.at
        pair = slice(None) if part is None else pl.ds(2 * part, 2)
        if half == 0:
            return (pair, (at.x + step) % 4, half)
        return ((at.z + step) % 4, pair, half)

    def start(self):
        at, kept = self.at, self.kept
        self.far, self.near = {}, []
        for half in range(2):
            for n, step in ((0, 3), (1, 1)):
                self.far[half, n] = at.send(
                    kept.at[self.block(half, 2, n)], self.early.at[half, n], self.along(half, False, step)
                )
        for half in range(2):
            for n, step in ((0, 3), (1, 1)):
                self.near.append(
                    at.send(
                        kept.at[self.block(half, step, 1 - n)],
                        self.landed.at[half, n, pl.ds(2 * (1 - n), 2)],
                        self.along(half, False, step),
                    )
                )

    def middle(self):
        at, kept = self.at, self.kept
        for half in range(2):
            for n, step in ((0, 3), (1, 1)):
                self.far[half, n].wait_recv()
                self.sums[half, n] = (
                    kept[self.block(half, step, n)].astype(F32) + self.early[half, n].astype(F32)
                ).astype(BF16)
                self.near.append(
                    at.send(
                        self.sums.at[half, n],
                        self.landed.at[half, n, pl.ds(2 * n, 2)],
                        self.along(half, False, step),
                    )
                )

    def second(self):
        at = self.at
        for copy in self.near:
            copy.wait_recv()
        self.last = []
        for half in range(2):
            self.four[half] = (
                self.kept[self.block(half, 0, None)].astype(F32)
                + self.landed[half, 0].astype(F32)
                + self.landed[half, 1].astype(F32)
            ).astype(BF16)
            here = at.z if half == 0 else at.x
            for n, step in enumerate((1, 3, 2)):
                self.last.append(
                    at.send(
                        self.four.at[half, (here + step) % 4],
                        self.parts.at[half, n],
                        self.along(half, True, step),
                    )
                )

    def reduce(self):
        at = self.at
        for copy in self.last:
            copy.wait_recv()
        for half in range(2):
            acc = self.four[half, at.z if half == 0 else at.x].astype(F32)
            for n in range(3):
                acc = acc + self.parts[half, n].astype(F32)
            self.total[half] = acc.astype(BF16)


def unit_rows(values):
    inverse = lax.rsqrt(jnp.mean(values * values, axis=-1, keepdims=True) + norm_eps)
    return values * inverse, inverse


def norm_back(gradient, unit, inverse, gain_vec):
    scaled = gradient * gain_vec
    inner_sum = jnp.mean(scaled * unit, axis=1, keepdims=True)
    return (
        inverse * (scaled - unit * inner_sum),
        jnp.sum(gradient * unit, axis=0, keepdims=True),
    )


def turn(x, cosine, sine):
    half = HEAD_DIM // 2
    lane = lax.broadcasted_iota(jnp.int32, x.shape, 1) % HEAD_DIM
    swapped = jnp.where(lane < half, pltpu.roll(x, 128 - half, 1), pltpu.roll(x, half, 1))
    return x * cosine + swapped * sine


def turn_all(x, cosine, sine):
    width = x.shape[1]
    pieces = []
    for first in range(0, width, 128):
        piece = x[:, first : min(first + 128, width)]
        if piece.shape[1] < 128:
            wide = jnp.concatenate([piece, jnp.zeros_like(piece)], axis=1)
            piece = turn(wide, cosine, sine)[:, : piece.shape[1]]
        else:
            piece = turn(piece, cosine, sine)
        pieces.append(piece)
    return jnp.concatenate(pieces, axis=1)


IN_NAMES = ("hidden", "ids_in", "freq", "attn_gain", "ffn_gain")
IN_NAMES += ("q_w", "k_w", "v_w", "o_w", "gate_w", "up_w", "down_w", "d_out")
OUT_NAMES = ("block_out", "input_grad", "attn_total", "kv_total", "ffn_total")
SCRATCH = dict(
    weights=((8, 400, HALF), BF16),
    o_parts=((2, 4, 4, 2, 2, 16, HALF), BF16),
    tokens=((2, OWN, D), BF16),
    own_o=((240, HALF), BF16),
    ids=((8, 16, OWN), BF16),
    normed_one=((2, OWN, HALF), BF16),
    bias=((OWN, KEYS), F32),
    cosine=((OWN, 128), F32),
    sine=((OWN, 128), F32),
    queries=((OWN, QD), BF16),
    kv=((8, OWN, 640), BF16),
    lse=((KV_HEADS, SHARE * OWN, 1), F32),
    attn=((OWN, QD), BF16),
    attn_halves=((2, OWN, HALF), BF16),
    attn_ring=((4, OWN, HALF), BF16),
    first_ring=((4, OWN, HALF), BF16),
    d_out_ring=((4, OWN, D), BF16),
    middle=((OWN, D), F32),
    normed_ring=((4, OWN, D), BF16),
    gate_up=((D, 2 * UNITS), BF16),
    down_parts=((2, 4, 4, 2, 16, UNITS), BF16),
    gate_land=((4, 4, 2, 16, 2 * UNITS), BF16),
    down=((D, UNITS), BF16),
    units=((4, OWN, UNITS), BF16),
    d_gate_up=((4, OWN, 2 * UNITS), BF16),
    ffn_parts=((4, 2, OWN // 2, D), BF16),
    ffn_early=((2, OWN // 2, D), BF16),
    ffn_sums=((2, OWN // 2, D), BF16),
    ffn_landed=((2, 2, OWN // 2, D), BF16),
    dn_parts=((4, 2, OWN // 2, D), BF16),
    dn_early=((2, OWN // 2, D), BF16),
    dn_sums=((2, OWN // 2, D), BF16),
    dn_landed=((2, 2, OWN // 2, D), BF16),
    ffn_halves=((2, 512, 1920), BF16),
    ffn_mate=((512, 1920), BF16),
    ffn_kept=((4, 4, 2, 16, 1920), BF16),
    ffn_far=((2, 2, 2, 16, 1920), BF16),
    ffn_pairs=((2, 2, 2, 16, 1920), BF16),
    ffn_near=((2, 2, 4, 16, 1920), BF16),
    ffn_four=((2, 4, 16, 1920), BF16),
    ffn_last=((2, 3, 16, 1920), BF16),
    ffn_sum=((2, 16, 1920), BF16),
    d_middle=((OWN, D), F32),
    d_y1_halves=((2, OWN, HALF), BF16),
    d_y1_ring=((4, OWN, HALF), BF16),
    d_kv=((8, OWN, 640), BF16),
    kv_mate=((4, OWN, 640), BF16),
    kv_parts=((4, 2, OWN // 2, 640), BF16),
    kv_early=((2, OWN // 2, 640), BF16),
    kv_sums=((2, OWN // 2, 640), BF16),
    kv_landed=((2, 2, OWN // 2, 640), BF16),
    d_q=((2, OWN, HALF), BF16),
    d_q_ring=((4, OWN, HALF), BF16),
    d_kv_own=((2, OWN, 320), BF16),
    d_kv_ring=((4, OWN, 320), BF16),
    gains=((4, 8, D), F32),
    qo_two=((2, 512, HALF), BF16),
    qo_mate=((512, HALF), BF16),
    qo_kept=((512, HALF), BF16),
    qo_ranks=((15, 32, HALF), BF16),
    qo_sum=((32, HALF), BF16),
    kv_two=((2, 512, 160), BF16),
    kv_grad_mate=((512, 160), BF16),
    kv_kept=((512, 160), BF16),
    kv_ranks=((15, 32, 160), BF16),
    kv_sum=((32, 160), BF16),
    send_sem=pltpu.SemaphoreType.DMA((SLOTS,)),
    recv_sem=pltpu.SemaphoreType.DMA((SLOTS,)),
)


def block_of(y, s):
    return ((y % 2) * 2 + s) * 2 + y // 2


def layer_kernel(*refs):
    names = IN_NAMES + OUT_NAMES + tuple(SCRATCH)
    m = dict(zip(names, refs))
    at = Place(m["send_sem"], m["recv_sem"])
    row, low, s, y, dp = at.row, at.low, at.s, at.y, at.dp
    mate = at.device(y, 1 - s)
    up_device, down_device = at.device(at.up, s), at.device(at.down, s)
    far_device, cross = at.device(at.far, s), at.device(at.far, 1 - s)
    mine = block_of(y, s)
    active = dp < CHUNKS
    not_ = jnp.logical_not

    at.greet()

    weights, ids = m["weights"], m["ids"]
    weights[mine, 0:240] = m["q_w"][...].T
    weights[mine, 240:320] = m["k_w"][...]
    weights[mine, 320:400] = m["v_w"][...]
    own_row = jnp.where(row == 0, m["ids_in"][:, 0:OWN], m["ids_in"][:, OWN:]).astype(F32)
    ids[mine] = jnp.broadcast_to(own_row, (16, OWN)).astype(BF16)
    m["own_o"][...] = m["o_w"][...].T
    at.meet()

    gate_up, o_parts, down_parts = m["gate_up"], m["o_parts"], m["down_parts"]
    o_slot, down_slot, gate_slot = at.slots(3), at.slots(2), at.slots(4)
    gate_mate_slot = at.slots(1)
    own_core = s == row
    strip = rows_of(dp, 16)

    def o_copy(n):
        other = (up_device, down_device, far_device)[n]
        return at.wire(m["own_o"].at[strip], o_parts.at[s, at.z, at.x, row, low], other, o_slot + n)

    def down_copy(r):
        target = r * 2 + row
        return target, at.wire(
            m["down_w"].at[strip, pl.ds(r * UNITS, UNITS)],
            down_parts.at[s, at.z, at.x, low],
            at.device(target, s),
            down_slot + r,
            down_slot + low,
        )

    def down_arrive(a):
        return low * 2 + a, at.wire(
            m["down_w"].at[strip, pl.ds(0, UNITS)],
            down_parts.at[s, at.z, at.x, a],
            up_device,
            down_slot + a,
        )

    gate_land = m["gate_land"]

    def gate_copy(n, part):
        source = (m["gate_w"], m["up_w"])[n]
        return at.wire(
            source.at[pl.ds(pl.multiple_of(dp * 32 + 16 * part, 16), 16)],
            gate_land.at[at.z, at.x, part, :, pl.ds(UNITS * n, UNITS)],
            cross,
            gate_slot + 2 * n + part,
        )

    gate_copies = [(n, part) for n in range(2) for part in range(2)]
    o_spread = Spread(at, o_parts.at[s])
    down_spread = Spread(at, down_parts.at[s])
    gate_spread = Spread(at, gate_land, not_(own_core))
    spreads = (o_spread, gate_spread, down_spread)

    def gate_mate(half):
        rows = pl.ds(pl.multiple_of(half * HALF, 32), HALF)
        return at.wire(gate_up.at[rows], gate_up.at[rows], mate, gate_mate_slot)

    @pl.when(active)
    def _():
        o_parts[s, at.z, at.x, row, low] = m["own_o"][strip]
        for n in range(3):
            o_copy(n).start()
        for r in range(2):
            target, copy = down_copy(r)

            @pl.when(target == y)
            def _():
                down_parts[s, at.z, at.x, low] = m["down_w"][strip, r * UNITS : (r + 1) * UNITS]

            @pl.when(target != y)
            def _():
                copy.start()

        @pl.when(not_(own_core))
        def _():
            for n, part in gate_copies:
                gate_copy(n, part).start()

    @pl.when(not_(active))
    def _():
        o_parts[s, at.z, at.x] = jnp.zeros((2, 2, 16, HALF), BF16)
        down_parts[s, at.z, at.x] = jnp.zeros((2, 16, UNITS), BF16)
        gate_land[at.z, at.x] = jnp.zeros((2, 16, 2 * UNITS), BF16)

    gather_w = Gather(at, weights, 400, 192, block_of)
    gather_w.start()
    ids_copies = [at.send(ids.at[mine], ids.at[mine], mate)]
    for other in (at.up, at.down, at.far):
        for core in (s, 1 - s):
            ids_copies.append(at.send(ids.at[mine], ids.at[mine], at.device(other, core)))

    @pl.when(own_core)
    def _():
        rows = pl.ds(pl.multiple_of(row * HALF, 32), HALF)
        gate_up[rows, 0:UNITS] = m["gate_w"][...]
        gate_up[rows, UNITS:] = m["up_w"][...]
        gate_mate(row).start()

    tokens_two, d_out_ring = m["tokens"], m["d_out_ring"]
    hidden, d_out = m["hidden"][...].T, m["d_out"][...].T
    tokens_two[0], tokens_two[1] = hidden[:OWN], hidden[OWN:]
    first_half = row == 0
    d_out_ring[0] = jnp.where(first_half, d_out[:OWN], d_out[OWN:])
    d_out_ring[3] = jnp.where(first_half, d_out[OWN:], d_out[:OWN])
    attn_gain, ffn_gain = m["attn_gain"][...], m["ffn_gain"][...]
    unit_one, _ = unit_rows(tokens_two[row].astype(F32))
    normed = (unit_one * attn_gain).astype(BF16)
    m["normed_one"][0] = normed[:, :HALF]
    m["normed_one"][1] = normed[:, HALF:]
    first_ring = m["first_ring"]
    first_ring[0] = m["normed_one"][row]
    unit_far, _ = unit_rows(tokens_two[1 - row].astype(F32))
    normed_far = (unit_far * attn_gain).astype(BF16)
    first_ring[3] = jnp.where(first_half, normed_far[:, :HALF], normed_far[:, HALF:])

    for copy in ids_copies:
        copy.wait_recv()
    own_ids = jnp.broadcast_to(own_row, (OWN, OWN)).T[:, 0:1].astype(jnp.int32)
    docs = jnp.concatenate([ids[b, 0:1, :] for b in range(8)], axis=1).astype(F32).astype(jnp.int32)
    earlier = jnp.sum((docs < own_ids).astype(F32), axis=1, keepdims=True)
    start = (low * 2 + s) * 256 + row * OWN
    position = start + lax.broadcasted_iota(jnp.int32, (OWN, 1), 0)
    angles = (position.astype(F32) - earlier) * m["freq"][...]
    lane = lax.broadcasted_iota(jnp.int32, (OWN, 128), 1) % HEAD_DIM
    sine = jnp.sin(angles)
    m["cosine"][...] = jnp.cos(angles)
    m["sine"][...] = jnp.where(lane < HEAD_DIM // 2, -sine, sine)
    key_at = lax.broadcasted_iota(jnp.int32, (OWN, KEYS), 1)
    allowed = (own_ids == docs) & (key_at <= position)
    m["bias"][...] = jnp.where(allowed, 0.0, -jnp.inf).astype(F32)

    @pl.when(active)
    def _():
        for n in range(3):
            o_copy(n).wait_recv()
        for a in range(2):
            source, copy = down_arrive(a)

            @pl.when(source != y)
            def _():
                copy.wait_recv()

        @pl.when(not_(own_core))
        def _():
            for n, part in gate_copies:
                gate_copy(n, part).wait_recv()

    for spread in spreads:
        spread.first()

    gather_w.relay()
    d_out_copies = [
        at.send(d_out_ring.at[0], d_out_ring.at[1], up_device),
        at.send(d_out_ring.at[0], d_out_ring.at[2], down_device),
    ]
    for spread in spreads:
        spread.second()
    gather_w.near()
    gather_w.finish()
    parts = []
    for c in range(4):
        part = dot_nt(m["normed_one"][0], weights[2 * c]) + dot_nt(m["normed_one"][1], weights[2 * c + 1])
        parts.append(part.astype(BF16).astype(F32))
    cosine, sine = m["cosine"][...], m["sine"][...]
    k = jnp.concatenate([part[:, 240:320] for part in parts], axis=1)
    v = jnp.concatenate([part[:, 320:400] for part in parts], axis=1)
    kv = m["kv"]
    kv[mine] = jnp.concatenate([turn_all(k, cosine, sine), v], axis=1).astype(BF16)
    gather_kv = Gather(at, kv, OWN, OWN // 2, block_of)
    gather_kv.start()
    q = jnp.concatenate([part[:, 0:240] for part in parts], axis=1)
    m["queries"][...] = turn_all(q, cosine, sine).astype(BF16)
    gather_kv.relay()
    for spread in spreads:
        spread.third()
    gather_kv.near()
    gather_kv.finish()

    o_spread.finish()
    o_mate = at.send(o_parts.at[s], o_parts.at[s], mate)

    for g in range(KV_HEADS):
        key = kv[:, :, g * HEAD_DIM : (g + 1) * HEAD_DIM].reshape(KEYS, HEAD_DIM)
        value = kv[:, :, KVD + g * HEAD_DIM : KVD + (g + 1) * HEAD_DIM].reshape(KEYS, HEAD_DIM)
        scores = dot_nt(heads_of(m["queries"], g), key) * SCALING
        scores = scores.reshape(SHARE, OWN, KEYS) + m["bias"][...][None]
        top = jnp.max(scores, axis=-1, keepdims=True)
        terms = jnp.exp(scores - top)
        total = jnp.sum(terms, axis=-1, keepdims=True)
        probs = (terms / total).astype(BF16).reshape(SHARE * OWN, KEYS)
        out = dot(probs, value).astype(BF16)
        for j in range(SHARE):
            head = (g * SHARE + j) * HEAD_DIM
            m["attn"][:, head : head + HEAD_DIM] = out[j * OWN : (j + 1) * OWN]
        m["lse"][g] = (top + jnp.log(total)).reshape(SHARE * OWN, 1)
    attn_halves = m["attn_halves"]
    attn_halves[0] = m["attn"][:, :HALF]
    attn_halves[1] = m["attn"][:, HALF:]
    o_mate.wait_recv()

    def o_block(r, c):
        return o_parts[c % 2, :, :, r, c // 2].reshape(256, HALF)[0:240]

    attn_out = [
        dot_nt(attn_halves[0], o_block(0, c)) + dot_nt(attn_halves[1], o_block(1, c)) for c in range(4)
    ]
    middle = tokens_two[row].astype(F32) + jnp.concatenate(attn_out, axis=1)
    m["middle"][...] = middle
    unit_two, _ = unit_rows(middle)
    ring = m["normed_ring"]
    ring[0] = (unit_two * ffn_gain).astype(BF16)
    gather_n = Gather(at, ring, OWN, OWN // 2)
    gather_n.start()

    gate_spread.finish()

    @pl.when(not_(own_core))
    def _():
        rows = pl.ds(pl.multiple_of((1 - row) * HALF, 32), HALF)
        gate_up[rows] = gate_land[...].reshape(512, 2 * UNITS)[0:HALF]
        gate_mate(1 - row).start()

    down_spread.finish()
    down_mate = at.send(down_parts.at[s], down_parts.at[s], mate)
    gather_n.relay()
    down_mate.wait_recv()
    for c in range(4):
        m["down"][c * 240 : (c + 1) * 240] = down_parts[c % 2, :, :, c // 2].reshape(256, UNITS)[0:240]
    for copy in d_out_copies:
        copy.wait_recv()
    gate_mate(row).wait_recv()

    ffn_parts, dn_parts = m["ffn_parts"], m["dn_parts"]

    def feed(p):
        gate_and_up = dot(ring[p], gate_up[...]).astype(BF16)
        gate, raise_ = gate_and_up[:, :UNITS].astype(F32), gate_and_up[:, UNITS:].astype(F32)
        sig = 1.0 / (1.0 + jnp.exp(-gate))
        silu = gate * sig
        unit = (silu * raise_).astype(BF16)
        m["units"][p] = unit
        d_unit = dot(d_out_ring[p], m["down"][...])
        d_gate = (d_unit * raise_ * sig * (1.0 + gate * (1.0 - sig))).astype(BF16)
        d_up = (d_unit * silu).astype(BF16)
        m["d_gate_up"][p] = jnp.concatenate([d_gate, d_up], axis=1)
        d_normed = dot_nt(m["d_gate_up"][p], gate_up[...]).astype(BF16)
        dn_parts[p] = d_normed.reshape(2, OWN // 2, D)

    def feed_out(p):
        ffn_parts[p] = dot_nt(m["units"][p], m["down"][...]).astype(BF16).reshape(2, OWN // 2, D)

    dn = Reduce(at, dn_parts, m["dn_early"], m["dn_sums"], m["dn_landed"])
    ffn = Reduce(at, ffn_parts, m["ffn_early"], m["ffn_sums"], m["ffn_landed"])
    feed(0)
    gather_n.near()
    feed(1)
    feed(2)
    gather_n.finish()
    feed(3)
    dn.start_far()
    dn.start_near()
    for p in (3, 1, 2):
        feed_out(p)
    dn.middle()
    ffn.start_far()
    ffn.start_near()
    feed_out(0)

    halves = m["ffn_halves"]
    tokens_n = ring[...].reshape(4 * OWN, D)
    d_gate_up = m["d_gate_up"][...].reshape(4 * OWN, 2 * UNITS)
    tokens_d = d_out_ring[...].reshape(4 * OWN, D)
    units = m["units"][...].reshape(4 * OWN, UNITS)
    for h in range(2):
        halves[h, 0:HALF, 0 : 2 * UNITS] = dot_tn(tokens_n[:, h * HALF : (h + 1) * HALF], d_gate_up).astype(BF16)
        grad = dot_tn(tokens_d[:, h * HALF : (h + 1) * HALF], units).astype(BF16)
        for i in range(CHUNKS):
            halves[h, 32 * i : 32 * i + 16, 2 * UNITS :] = grad[16 * i : 16 * i + 16]
            halves[h, 32 * i + 16 : 32 * i + 32, 2 * UNITS :] = grad[240 + 16 * i : 256 + 16 * i]
        halves[h, HALF:, :] = jnp.zeros((32, 1920), BF16)
    ffn_pair = at.send(halves.at[1 - s], m["ffn_mate"], mate)
    ffn_collect = Collect(
        at,
        m["ffn_kept"],
        m["ffn_far"],
        m["ffn_pairs"],
        m["ffn_near"],
        m["ffn_four"],
        m["ffn_last"],
        m["ffn_sum"],
    )

    d_normed = dn.finish()
    ffn.middle()
    middle = m["middle"][...]
    unit_two, inverse_two = unit_rows(middle)
    d_middle, ffn_gain_part = norm_back(d_normed, unit_two, inverse_two, ffn_gain)
    d_middle = d_middle + d_out_ring[0].astype(F32)
    m["d_middle"][...] = d_middle
    d_y1 = d_middle.astype(BF16)
    d_y1_halves, d_y1_ring = m["d_y1_halves"], m["d_y1_ring"]
    d_y1_halves[0] = d_y1[:, :HALF]
    d_y1_halves[1] = d_y1[:, HALF:]
    ffn_pair.wait_recv()
    for z in range(4):
        for x in range(4):
            rows = pl.ds(32 * (4 * z + x), 32)
            both = halves[s, rows].astype(F32) + m["ffn_mate"][rows].astype(F32)
            m["ffn_kept"][z, x] = both.astype(BF16).reshape(2, 16, 1920)
    ffn_collect.start()
    d_attn = [0.0, 0.0]
    for c in range(4):
        for r in range(2):
            d_attn[r] = d_attn[r] + dot(d_y1[:, c * 240 : (c + 1) * 240], o_block(r, c))
    d_attn = jnp.concatenate(d_attn, axis=1).astype(BF16)

    up_low, up_row, down_row = 1 - low, at.up // 2, at.down // 2
    attn_ring, first_send = m["attn_ring"], m["normed_one"]
    side_copies = [
        at.send(d_y1_halves.at[up_low], d_y1_ring.at[1], up_device),
        at.send(d_y1_halves.at[up_low], d_y1_ring.at[2], down_device),
        at.send(attn_halves.at[up_row], attn_ring.at[1], up_device),
        at.send(attn_halves.at[down_row], attn_ring.at[2], down_device),
        at.send(first_send.at[up_row], first_ring.at[1], up_device),
        at.send(first_send.at[down_row], first_ring.at[2], down_device),
        at.send(attn_halves.at[1 - row], attn_ring.at[3], far_device),
        at.send(d_y1_halves.at[low], d_y1_ring.at[3], far_device),
    ]
    attn_ring[0] = attn_halves[row]
    d_y1_ring[0] = d_y1_halves[low]

    d_kv = m["d_kv"]
    d_q = []
    for g in range(KV_HEADS):
        own = slice(g * HEAD_DIM, (g + 1) * HEAD_DIM)
        val = slice(KVD + g * HEAD_DIM, KVD + (g + 1) * HEAD_DIM)
        key = kv[:, :, own].reshape(KEYS, HEAD_DIM)
        value = kv[:, :, val].reshape(KEYS, HEAD_DIM)
        query, d_head = heads_of(m["queries"], g), heads_of(d_attn, g)
        scores = dot_nt(query, key) * SCALING
        scores = scores.reshape(SHARE, OWN, KEYS) + m["bias"][...][None]
        probs = jnp.exp(scores.reshape(SHARE * OWN, KEYS) - m["lse"][g])
        d_probs = dot_nt(d_head, value)
        inner = jnp.sum(probs * d_probs, axis=-1, keepdims=True)
        d_scores = (probs * (d_probs - inner)).astype(BF16)
        d_query = dot(d_scores, key) * SCALING
        d_q += [d_query[j * OWN : (j + 1) * OWN] for j in range(SHARE)]
        d_kv[:, :, own] = (dot_tn(d_scores, query) * SCALING).astype(BF16).reshape(8, OWN, HEAD_DIM)
        d_kv[:, :, val] = dot_tn(probs.astype(BF16), d_head).astype(BF16).reshape(8, OWN, HEAD_DIM)
        if g == 2:
            ffn_collect.middle()

    ffn_collect.second()
    kv_copies = []
    order = ((3, at.far), (1, at.down), (2, at.up), (0, y))
    for p, t in order:
        kv_copies.append(at.send(d_kv.at[block_of(t, 1 - s)], m["kv_mate"].at[p], mate))
    cosine, sine = m["cosine"][...], -m["sine"][...]
    d_q = turn_all(jnp.concatenate(d_q, axis=1), cosine, sine).astype(BF16)
    kv_sum = Reduce(at, m["kv_parts"], m["kv_early"], m["kv_sums"], m["kv_landed"])
    for (p, t), copy in zip(order, kv_copies):
        copy.wait_recv()
        both = d_kv[block_of(t, s)].astype(F32) + m["kv_mate"][p].astype(F32)
        m["kv_parts"][p] = both.astype(BF16).reshape(2, OWN // 2, 640)
        if p == 3:
            kv_sum.start_far()
        if p == 2:
            kv_sum.start_near()
    d_q_two, d_q_ring = m["d_q"], m["d_q_ring"]
    d_q_two[0], d_q_two[1] = d_q[:, :HALF], d_q[:, HALF:]
    kv_sum.middle()
    q_copies = [
        at.send(d_q_two.at[up_low], d_q_ring.at[1], up_device),
        at.send(d_q_two.at[up_low], d_q_ring.at[2], down_device),
        at.send(d_q_two.at[low], d_q_ring.at[3], far_device),
    ]
    d_q_ring[0] = d_q_two[low]
    d_normed_one = [0.0, 0.0]
    for c in range(4):
        for r in range(2):
            d_normed_one[r] = d_normed_one[r] + dot(d_q[:, c * 240 : (c + 1) * 240], weights[2 * c + r, 0:240])

    ffn_collect.reduce()
    sums, ffn_total = m["ffn_sum"], m["ffn_total"]
    gate_back_slot, back_slot = at.slots(1), at.slots(2)
    own_rows = rows_of(dp, 32)
    lanes = pl.ds(2 * UNITS, UNITS)
    owner = low * 2 + s

    def gate_back():
        both = pl.ds(0, 2 * UNITS)
        return at.wire(
            sums.at[:, :, both], ffn_total.at[at.z, at.x, :, :, both], cross, gate_back_slot
        )

    def down_back(j):
        return at.wire(
            sums.at[j, :, lanes],
            ffn_total.at[at.z, at.x, row, :, lanes],
            at.device(owner, j),
            back_slot + j,
            back_slot + row,
        )

    @pl.when(own_core)
    def _():
        ffn_total[at.z, at.x, :, :, 0 : 2 * UNITS] = sums[:, :, 0 : 2 * UNITS]

    @pl.when(not_(own_core))
    def _():
        gate_back().start()

    for j in range(2):
        here = (owner == y) & (s == j)
        copy = down_back(j)

        @pl.when(here)
        def _():
            ffn_total[at.z, at.x, row, :, 2 * UNITS :] = sums[j, :, 2 * UNITS :]

        @pl.when(not_(here))
        def _():
            copy.start()

    d_kv_sum = kv_sum.finish()
    d_k = turn_all(d_kv_sum[:, :KVD], cosine, sine).astype(BF16)
    d_v = d_kv_sum[:, KVD:].astype(BF16)
    d_kv_own, d_kv_ring = m["d_kv_own"], m["d_kv_ring"]
    for a in range(2):
        d_kv_own[a] = jnp.concatenate(
            [d_k[:, a * 160 : (a + 1) * 160], d_v[:, a * 160 : (a + 1) * 160]], axis=1
        )
    kv_out = [
        at.send(d_kv_own.at[up_low], d_kv_ring.at[1], up_device),
        at.send(d_kv_own.at[up_low], d_kv_ring.at[2], down_device),
        at.send(d_kv_own.at[low], d_kv_ring.at[3], far_device),
    ]
    d_kv_ring[0] = d_kv_own[low]

    for c in range(4):
        piece = jnp.concatenate(
            [d_k[:, c * 80 : (c + 1) * 80], d_v[:, c * 80 : (c + 1) * 80]], axis=1
        )
        for r in range(2):
            d_normed_one[r] = d_normed_one[r] + dot(piece, weights[2 * c + r, 240:400])
    unit_one, inverse_one = unit_rows(tokens_two[row].astype(F32))
    d_tokens, attn_gain_part = norm_back(
        jnp.concatenate(d_normed_one, axis=1), unit_one, inverse_one, attn_gain
    )
    gains = m["gains"]
    gains[0] = jnp.concatenate([attn_gain_part, ffn_gain_part, jnp.zeros((6, D), F32)], axis=0)
    gain_copies = [
        at.send(gains.at[0], gains.at[1], up_device),
        at.send(gains.at[0], gains.at[2], down_device),
        at.send(gains.at[0], gains.at[3], far_device),
    ]
    input_grad = m["input_grad"]
    input_grad[row] = (d_tokens + m["d_middle"][...]).astype(BF16)

    @pl.when(not_(own_core))
    def _():
        gate_back().wait_recv()

    for r in range(2):
        source = r * 2 + row

        @pl.when(not_((source == y) & (low == s)))
        def _():
            at.wire(
                sums.at[0, :, lanes],
                ffn_total.at[at.z, at.x, r, :, lanes],
                mate,
                back_slot + r,
            ).wait_recv()

    ffn_spread = Spread(at, ffn_total)
    ffn_spread.first()

    for copy in side_copies + q_copies:
        copy.wait_recv()
    first_all = first_ring[...].reshape(4 * OWN, HALF)
    q_grad = dot_tn(first_all, d_q_ring[...].reshape(4 * OWN, HALF)).astype(BF16)
    o_grad = dot_tn(
        attn_ring[...].reshape(4 * OWN, HALF), d_y1_ring[...].reshape(4 * OWN, HALF)
    ).astype(BF16)
    qo_two = m["qo_two"]
    for b in range(2):
        pick = slice(b * 240, (b + 1) * 240)
        qo_two[b, 0:HALF, :] = jnp.concatenate([q_grad[:, pick], o_grad[:, pick]], axis=1)
        qo_two[b, HALF:, :] = jnp.zeros((32, HALF), BF16)
    qo_ranks = RankSum(
        at, qo_two, m["qo_mate"], m["qo_kept"], m["qo_ranks"], m["qo_sum"], m["attn_total"]
    )
    ffn_spread.second()
    qo_ranks.start()

    for copy in kv_out + gain_copies:
        copy.wait_recv()
    kv_grad = dot_tn(first_all, d_kv_ring[...].reshape(4 * OWN, 320)).astype(BF16)
    gain_sum = (gains[0] + gains[1] + gains[2] + gains[3])[0:2].astype(BF16)
    gain_rows = [gain_sum[g : g + 1, p * 160 : (p + 1) * 160] for g in range(2) for p in range(6)]
    gain_block = jnp.concatenate(gain_rows + [jnp.zeros((20, 160), BF16)], axis=0)
    kv_two = m["kv_two"]
    for b in range(2):
        kv_two[b, 0:HALF, :] = jnp.concatenate(
            [kv_grad[:, b * 80 : (b + 1) * 80], kv_grad[:, 160 + b * 80 : 160 + (b + 1) * 80]], axis=1
        )
        kv_two[b, HALF:, :] = gain_block
    kv_ranks = RankSum(
        at, kv_two, m["kv_grad_mate"], m["kv_kept"], m["kv_ranks"], m["kv_sum"], m["kv_total"]
    )
    kv_ranks.start()
    qo_ranks.scatter()
    ffn_spread.third()
    kv_ranks.scatter()

    block_out = m["block_out"]
    block_out[row] = (m["middle"][...] + ffn.finish()).astype(BF16)
    out_copies = [
        at.send(block_out.at[row], block_out.at[row], far_device),
        at.send(input_grad.at[row], input_grad.at[row], far_device),
    ]

    qo_ranks.reduce()
    m["attn_total"][own_rows] = m["qo_sum"][...]
    qo_ranks.gather()
    kv_ranks.reduce()
    m["kv_total"][own_rows] = m["kv_sum"][...]
    kv_ranks.gather()
    for copy in out_copies:
        copy.wait_recv()
    ffn_spread.finish()
    qo_ranks.finish()
    kv_ranks.finish()

    for copy in at.open:
        copy.wait_send()
    gate_mate(row).wait_send()
    for spread in spreads + (ffn_spread,):
        spread.drain()

    @pl.when(active)
    def _():
        for n in range(3):
            o_copy(n).wait_send()
        for r in range(2):
            target, copy = down_copy(r)

            @pl.when(target != y)
            def _():
                copy.wait_send()

        @pl.when(not_(own_core))
        def _():
            for n, part in gate_copies:
                gate_copy(n, part).wait_send()

    @pl.when(not_(own_core))
    def _():
        gate_back().wait_send()

    for j in range(2):
        copy = down_back(j)

        @pl.when(not_((owner == y) & (s == j)))
        def _():
            copy.wait_send()


def results_kernel(*refs):
    ins, outs, held, sems = refs[:5], refs[5:16], refs[16:21], refs[21]
    copies = [
        pltpu.make_async_copy(src, dst, sems.at[n]) for n, (src, dst) in enumerate(zip(ins, held))
    ]
    for copy in copies:
        copy.start()
    block_in, input_in, attn_in, kv_in, ffn_in = held
    block, inputs, attn_gain, q_grad, k_grad, v_grad, o_grad, ffn_gain, gate, raise_, down = outs
    for copy in copies:
        copy.wait()
    block[...] = block_in[...].reshape(2 * OWN, D).astype(F32).T
    inputs[...] = input_in[...].reshape(2 * OWN, D).astype(F32).T
    q_grad[...] = attn_in[0:HALF, 0:240].astype(F32)
    o_grad[...] = attn_in[0:HALF, 240:480].astype(F32)
    kv_grad = kv_in[0:HALF, :].astype(F32).T
    k_grad[...] = kv_grad[0:80]
    v_grad[...] = kv_grad[80:160]
    gains = kv_in[HALF:512, :].astype(F32)
    for p in range(6):
        attn_gain[:, p * 160 : (p + 1) * 160] = gains[p : p + 1]
        ffn_gain[:, p * 160 : (p + 1) * 160] = gains[6 + p : 7 + p]
    gate[...] = ffn_in[0:CHUNKS, :, :, 0:UNITS].reshape(HALF, UNITS).astype(F32)
    raise_[...] = ffn_in[0:CHUNKS, :, :, UNITS : 2 * UNITS].reshape(HALF, UNITS).astype(F32)
    for i in range(CHUNKS):
        for r in range(2):
            down[16 * i : 16 * i + 16, r * UNITS : (r + 1) * UNITS] = ffn_in[
                i, r, :, 2 * UNITS :
            ].astype(F32)


def shards(
    hidden_in,
    segment_ids,
    attn_gain,
    q_weight,
    k_weight,
    v_weight,
    o_weight,
    ffn_gain,
    gate_weight,
    up_weight,
    down_weight,
    d_out,
):
    frequency = np.float32(rope_base) ** (-np.arange(HEAD_DIM // 2, dtype=np.float32) * 2 / HEAD_DIM)
    freq = jnp.asarray(np.tile(frequency.astype(np.float32), 4)[None, :])
    scratch = [
        pltpu.VMEM(*kind) if isinstance(kind, tuple) else kind for kind in SCRATCH.values()
    ]
    local = pl.BlockSpec(memory_space=pltpu.VMEM)
    kept = pl.pallas_call(
        layer_kernel,
        out_shape=[
            jax.ShapeDtypeStruct((2, OWN, D), BF16),
            jax.ShapeDtypeStruct((2, OWN, D), BF16),
            jax.ShapeDtypeStruct((512, HALF), BF16),
            jax.ShapeDtypeStruct((512, 160), BF16),
            jax.ShapeDtypeStruct((4, 4, 2, 16, 1920), BF16),
        ],
        in_specs=[local] * len(IN_NAMES),
        out_specs=[local] * len(OUT_NAMES),
        scratch_shapes=scratch,
        compiler_params=pltpu.CompilerParams(
            collective_id=1, has_side_effects=True, vmem_limit_bytes=60 * 1024 * 1024
        ),
    )(
        hidden_in.T,
        segment_ids[None, :],
        freq,
        attn_gain[None, :],
        ffn_gain[None, :],
        q_weight,
        k_weight.T,
        v_weight.T,
        o_weight,
        gate_weight,
        up_weight,
        down_weight.T,
        d_out.T,
    )
    shapes = [
        (D, 2 * OWN), (D, 2 * OWN), (1, D), (HALF, 240), (80, HALF), (80, HALF),
        (HALF, 240), (1, D), (HALF, UNITS), (HALF, UNITS), (240, 2 * UNITS),
    ]
    outs = pl.pallas_call(
        results_kernel,
        out_shape=[jax.ShapeDtypeStruct(shape, F32) for shape in shapes],
        in_specs=[pl.BlockSpec(memory_space=pl.ANY)] * len(OUT_NAMES),
        out_specs=[local] * len(shapes),
        scratch_shapes=[
            pltpu.VMEM((2, OWN, D), BF16),
            pltpu.VMEM((2, OWN, D), BF16),
            pltpu.VMEM((512, HALF), BF16),
            pltpu.VMEM((512, 160), BF16),
            pltpu.VMEM((16, 2, 16, 1920), BF16),
            pltpu.SemaphoreType.DMA((5,)),
        ],
        compiler_params=pltpu.CompilerParams(vmem_limit_bytes=62 * 1024 * 1024),
    )(*kept[:4], kept[4].reshape(16, 2, 16, 1920))
    turned = (0, 1, 4, 5, 10)
    outs = [out.T if i in turned else out for i, out in enumerate(outs)]
    outs[2], outs[7] = outs[2].reshape(D), outs[7].reshape(D)
    return tuple(outs)


def solution(mesh):
    rows, blocks = P(("dp", "col"), None), P("row", "col")
    return jax.shard_map(
        shards,
        mesh=mesh,
        in_specs=(
            rows, P(("dp", "col")), P(), blocks, blocks, blocks, blocks, P(), blocks, blocks, blocks, rows,
        ),
        out_specs=(rows, rows, P(), blocks, blocks, blocks, blocks, P(), blocks, blocks, blocks),
        check_vma=False,
    )
```

time: 877 us -> 158 us (0.18)
  blocking collectives: 419 us -> 0 us
  waiting for transfers between devices: 277 us -> 0 us
  Pallas kernels: 0 us -> 157 us
  matrix products: 71 us -> 0 us
  other arithmetic: 43.4 us -> 0 us
  local copies, waits for them, and re-layouts: 34.9 us -> 0 us
  between operations: 16.1 us -> 0.84 us
  starting transfers between devices: 12.6 us -> 0 us
    psum x4 -> x0, blocking collectives: 218 us -> none  [the longest x2 172 us: forward_project(): result = lax.psum(arrived, 'row')]
    pallas_call x0 -> x2, Pallas kernels: none -> 157 us  [the longest x1 151 us: shards(): pl.pallas_call(layer_kernel, out_shape=[jax.ShapeDtypeStruct((2, OWN, D),...]
    psum x3 -> x0, waiting for transfers between devices: 113 us -> none  [the longest x1 72.7 us: shards(): lax.psum(qkv_grad.astype(jnp.bfloat16), 'dp').astype(jnp.float32)]
    all_gather x9 -> x0, blocking collectives: 103 us -> none  [the longest x3 37.6 us: backward_project(): lax.all_gather(share_half.astype(jnp.bfloat16), 'row', axis=1, tiled=True)]
    all_to_all x5 -> x0, blocking collectives: 98.3 us -> none  [the longest x3 59.2 us: backward_project(): lax.all_to_all(gradient, 'col', split_axis=1, concat_axis=0, tiled=True)]
    all_to_all x3 -> x0, waiting for transfers between devices: 80.6 us -> none  [the longest x2 72.7 us: forward_project(): lax.all_to_all(partial_out, 'col', split_axis=0, concat_axis=1, tiled=True)]
    dot_general x18 -> x0, matrix products: 71 us -> none  [the longest x1 12.8 us: shards(): jnp.einsum('qkgd,pkd->kgqp', d_attn, values_all, preferred_element_type=j...]
    reduce_scatter x6 -> x0, waiting for transfers between devices: 64.2 us -> none  [the longest x4 39.8 us: backward_project(): lax.psum_scatter(lax.dot_general(grad_cols, weight_block, (((1,), (1,)),...]
  transfers between devices with their start and end apart: 14 -> 0, of which waited for: 9 -> 0; matrix products, arithmetic and copies ran while one was open for 7% -> 0% of each run, Pallas kernels for 0% -> 0%
where the time goes in v1:
time: 158 us; the launch traced here: 157 us
  Pallas kernels  157 us (99%)
    pallas_call x1, Pallas kernels, shards(): pl.pallas_call(layer_kernel, out_shape=[jax.ShapeDtypeStruct((2, OWN, D),...  151 us
    pallas_call x1, Pallas kernels, shards(): pl.pallas_call(results_kernel, out_shape=[jax.ShapeDtypeStruct(shape, F32...  5.52 us

profile of v1, /device:TPU:0, one launch (start us, length us, event | category | flops | bytes accessed | tf_op | source)
XLA Modules:
  0.0 157.4 jit_solution(10025336750979507727)
XLA Ops:
  0.6 151.0 %shard_map.212 = (bf16[2,128,960]{2,1,0:T(8,128)(2,1)}, bf16[2,128,960]{2,1,0:T(8,128)(2,1)}, bf16[512,480]{1,0:T(8,128)(2,1)}, bf16[512,160]{1,0:T(8,128)(2,1)}, bf16[4,4,2,16,1920]{4,3,2,1,0:T(8,128)(2,1)}) custom-call(bf16[960,256]{1,0:T(8,128)(2,1)} %bitcast.18, s32[1,256]{1,0:T(1,128)} %bitcast.24, f32[1,128]{1,0:T(1,128)} %constant.2.clone.refs_2_, ...), custom_call_target="tpu_custom_call" | custom-call | tf_op jit(solution)/shard_map/pallas_call | solution.py:1166
  151.7 5.5 %shard_map.213 = (f32[960,256]{1,0:T(8,128)}, f32[960,256]{1,0:T(8,128)}, f32[1,960]{1,0:T(1,128)}, f32[480,240]{1,0:T(8,128)}, f32[80,480]{1,0:T(8,128)}, /*ind...) custom-call(bf16[2,128,960]{2,1,0:T(8,128)(2,1)} %get-tuple-element., ...), custom_call_target="tpu_custom_call" | custom-call | tf_op jit(solution)/shard_map/pallas_call | solution.py:1200

commit v2 on v1

--- a/solution.py
+++ b/solution.py
@@ -1,3 +1,5 @@
+import types
+
 import jax
 import jax.numpy as jnp
 import numpy as np
@@ -195,52 +197,27 @@
         return total.reshape(total.shape[0] * total.shape[1], total.shape[2])
 
 
-class RankSum:
-    def __init__(self, at, halves, mate, kept, parts, total, out):
-        self.at, self.halves, self.mate, self.kept = at, halves, mate, kept
-        self.parts, self.total, self.out = parts, total, out
-
-    def start(self):
+class Far:
+    def __init__(self, at, src, on_up, on_down, relay):
+        self.at, self.src, self.on_up, self.on_down, self.buf = at, src, on_up, on_down, relay
+        self.up_device, self.down_device = at.device(at.up, at.s), at.device(at.down, at.s)
+        self.low, self.high = pl.ds(0, OWN // 2), pl.ds(OWN // 2, OWN // 2)
+
+    def first(self):
         at = self.at
-        self.swap = at.send(self.halves.at[1 - at.s], self.mate, at.device(at.y, 1 - at.s))
-
-    def join(self):
+        self.to_up = at.send(self.src.at[self.low], self.buf.at[0], self.up_device)
+        self.to_down = at.send(self.src.at[self.high], self.buf.at[1], self.down_device)
+
+    def relay(self):
         at = self.at
-        self.swap.wait_recv()
-
-        def add(i, carry):
-            rows = rows_of(i, 32)
-            self.kept[rows] = (
-                self.halves[at.s, rows].astype(F32) + self.mate[rows].astype(F32)
-            ).astype(BF16)
-            return carry
-
-        lax.fori_loop(0, 16, add, 0)
-
-    def scatter(self):
-        at = self.at
-        self.join()
-        self.copies = [
-            at.send(self.kept.at[rows_of((at.dp + k) % at.ranks, 32)], self.parts.at[k - 1], at.peer(k))
-            for k in range(1, at.ranks)
-        ]
-
-    def reduce(self):
-        at = self.at
-        acc = self.kept[rows_of(at.dp, 32)].astype(F32)
-        for k, copy in enumerate(self.copies):
-            copy.wait_recv()
-            acc = acc + self.parts[k].astype(F32)
-        self.total[...] = acc.astype(BF16)
-
-    def gather(self):
-        at = self.at
-        own = self.out.at[rows_of(at.dp, 32)]
-        self.back = [at.send(own, own, at.peer(k)) for k in range(1, at.ranks)]
+        self.to_up.wait_recv()
+        self.last_up = at.send(self.buf.at[0], self.on_up.at[self.low], self.up_device)
+        self.to_down.wait_recv()
+        self.last_down = at.send(self.buf.at[1], self.on_down.at[self.high], self.down_device)
 
     def finish(self):
-        for copy in self.back:
-            copy.wait_recv()
+        self.last_up.wait_recv()
+        self.last_down.wait_recv()
 
 
 class Spread:
@@ -451,7 +428,6 @@
 
 IN_NAMES = ("hidden", "ids_in", "freq", "attn_gain", "ffn_gain")
 IN_NAMES += ("q_w", "k_w", "v_w", "o_w", "gate_w", "up_w", "down_w", "d_out")
-OUT_NAMES = ("block_out", "input_grad", "attn_total", "kv_total", "ffn_total")
 SCRATCH = dict(
     weights=((8, 400, HALF), BF16),
     o_parts=((2, 4, 4, 2, 2, 16, HALF), BF16),
@@ -511,14 +487,26 @@
     gains=((4, 8, D), F32),
     qo_two=((2, 512, HALF), BF16),
     qo_mate=((512, HALF), BF16),
-    qo_kept=((512, HALF), BF16),
-    qo_ranks=((15, 32, HALF), BF16),
-    qo_sum=((32, HALF), BF16),
     kv_two=((2, 512, 160), BF16),
     kv_grad_mate=((512, 160), BF16),
-    kv_kept=((512, 160), BF16),
-    kv_ranks=((15, 32, 160), BF16),
-    kv_sum=((32, 160), BF16),
+    attn_kept=((4, 4, 2, 16, 640), BF16),
+    attn_far=((2, 2, 2, 16, 640), BF16),
+    attn_pairs=((2, 2, 2, 16, 640), BF16),
+    attn_near=((2, 2, 4, 16, 640), BF16),
+    attn_four=((2, 4, 16, 640), BF16),
+    attn_last=((2, 3, 16, 640), BF16),
+    attn_sum=((2, 16, 640), BF16),
+    attn_relay=((2, OWN // 2, HALF), BF16),
+    d_y1_relay=((2, OWN // 2, HALF), BF16),
+    d_q_relay=((2, OWN // 2, HALF), BF16),
+    d_kv_relay=((2, OWN // 2, 320), BF16),
+    block_relay=((2, OWN // 2, D), BF16),
+    input_relay=((2, OWN // 2, D), BF16),
+    block_out=((2, OWN, D), BF16),
+    input_grad=((2, OWN, D), BF16),
+    attn_total=((4, 4, 2, 16, 640), BF16),
+    ffn_total=((4, 4, 2, 16, 1920), BF16),
+    out_sem=pltpu.SemaphoreType.DMA((4,)),
     send_sem=pltpu.SemaphoreType.DMA((SLOTS,)),
     recv_sem=pltpu.SemaphoreType.DMA((SLOTS,)),
 )
@@ -529,9 +517,17 @@
 
 
 def layer_kernel(*refs):
-    names = IN_NAMES + OUT_NAMES + tuple(SCRATCH)
-    m = dict(zip(names, refs))
-    at = Place(m["send_sem"], m["recv_sem"])
+    count = len(IN_NAMES)
+    outs, refs = refs[count : count + 4], refs[:count] + refs[count + 4 :]
+    m = types.SimpleNamespace(**dict(zip(IN_NAMES + tuple(SCRATCH), refs)))
+    leaving = []
+
+    def leave(n, src):
+        copy = pltpu.make_async_copy(src, outs[n], m.out_sem.at[n])
+        copy.start()
+        leaving.append(copy)
+
+    at = Place(m.send_sem, m.recv_sem)
     row, low, s, y, dp = at.row, at.low, at.s, at.y, at.dp
     mate = at.device(y, 1 - s)
     up_device, down_device = at.device(at.up, s), at.device(at.down, s)
@@ -542,16 +538,16 @@
 
     at.greet()
 
-    weights, ids = m["weights"], m["ids"]
-    weights[mine, 0:240] = m["q_w"][...].T
-    weights[mine, 240:320] = m["k_w"][...]
-    weights[mine, 320:400] = m["v_w"][...]
-    own_row = jnp.where(row == 0, m["ids_in"][:, 0:OWN], m["ids_in"][:, OWN:]).astype(F32)
+    weights, ids = m.weights, m.ids
+    weights[mine, 0:240] = m.q_w[...].T
+    weights[mine, 240:320] = m.k_w[...]
+    weights[mine, 320:400] = m.v_w[...]
+    own_row = jnp.where(row == 0, m.ids_in[:, 0:OWN], m.ids_in[:, OWN:]).astype(F32)
     ids[mine] = jnp.broadcast_to(own_row, (16, OWN)).astype(BF16)
-    m["own_o"][...] = m["o_w"][...].T
+    m.own_o[...] = m.o_w[...].T
     at.meet()
 
-    gate_up, o_parts, down_parts = m["gate_up"], m["o_parts"], m["down_parts"]
+    gate_up, o_parts, down_parts = m.gate_up, m.o_parts, m.down_parts
     o_slot, down_slot, gate_slot = at.slots(3), at.slots(2), at.slots(4)
     gate_mate_slot = at.slots(1)
     own_core = s == row
@@ -559,12 +555,12 @@
 
     def o_copy(n):
         other = (up_device, down_device, far_device)[n]
-        return at.wire(m["own_o"].at[strip], o_parts.at[s, at.z, at.x, row, low], other, o_slot + n)
+        return at.wire(m.own_o.at[strip], o_parts.at[s, at.z, at.x, row, low], other, o_slot + n)
 
     def down_copy(r):
         target = r * 2 + row
         return target, at.wire(
-            m["down_w"].at[strip, pl.ds(r * UNITS, UNITS)],
+            m.down_w.at[strip, pl.ds(r * UNITS, UNITS)],
             down_parts.at[s, at.z, at.x, low],
             at.device(target, s),
             down_slot + r,
@@ -573,16 +569,16 @@
 
     def down_arrive(a):
         return low * 2 + a, at.wire(
-            m["down_w"].at[strip, pl.ds(0, UNITS)],
+            m.down_w.at[strip, pl.ds(0, UNITS)],
             down_parts.at[s, at.z, at.x, a],
             up_device,
             down_slot + a,
         )
 
-    gate_land = m["gate_land"]
+    gate_land = m.gate_land
 
     def gate_copy(n, part):
-        source = (m["gate_w"], m["up_w"])[n]
+        source = (m.gate_w, m.up_w)[n]
         return at.wire(
             source.at[pl.ds(pl.multiple_of(dp * 32 + 16 * part, 16), 16)],
             gate_land.at[at.z, at.x, part, :, pl.ds(UNITS * n, UNITS)],
@@ -600,33 +596,6 @@
         rows = pl.ds(pl.multiple_of(half * HALF, 32), HALF)
         return at.wire(gate_up.at[rows], gate_up.at[rows], mate, gate_mate_slot)
 
-    @pl.when(active)
-    def _():
-        o_parts[s, at.z, at.x, row, low] = m["own_o"][strip]
-        for n in range(3):
-            o_copy(n).start()
-        for r in range(2):
-            target, copy = down_copy(r)
-
-            @pl.when(target == y)
-            def _():
-                down_parts[s, at.z, at.x, low] = m["down_w"][strip, r * UNITS : (r + 1) * UNITS]
-
-            @pl.when(target != y)
-            def _():
-                copy.start()
-
-        @pl.when(not_(own_core))
-        def _():
-            for n, part in gate_copies:
-                gate_copy(n, part).start()
-
-    @pl.when(not_(active))
-    def _():
-        o_parts[s, at.z, at.x] = jnp.zeros((2, 2, 16, HALF), BF16)
-        down_parts[s, at.z, at.x] = jnp.zeros((2, 16, UNITS), BF16)
-        gate_land[at.z, at.x] = jnp.zeros((2, 16, 2 * UNITS), BF16)
-
     gather_w = Gather(at, weights, 400, 192, block_of)
     gather_w.start()
     ids_copies = [at.send(ids.at[mine], ids.at[mine], mate)]
@@ -634,29 +603,58 @@
         for core in (s, 1 - s):
             ids_copies.append(at.send(ids.at[mine], ids.at[mine], at.device(other, core)))
 
+    @pl.when(active)
+    def _():
+        o_parts[s, at.z, at.x, row, low] = m.own_o[strip]
+        for n in range(3):
+            o_copy(n).start()
+        for r in range(2):
+            target, copy = down_copy(r)
+
+            @pl.when(target == y)
+            def _():
+                down_parts[s, at.z, at.x, low] = m.down_w[strip, r * UNITS : (r + 1) * UNITS]
+
+            @pl.when(target != y)
+            def _():
+                copy.start()
+
+        @pl.when(not_(own_core))
+        def _():
+            for n, part in gate_copies:
+                gate_copy(n, part).start()
+
+    @pl.when(not_(active))
+    def _():
+        o_parts[s, at.z, at.x] = jnp.zeros((2, 2, 16, HALF), BF16)
+        down_parts[s, at.z, at.x] = jnp.zeros((2, 16, UNITS), BF16)
+        gate_land[at.z, at.x] = jnp.zeros((2, 16, 2 * UNITS), BF16)
+
     @pl.when(own_core)
     def _():
         rows = pl.ds(pl.multiple_of(row * HALF, 32), HALF)
-        gate_up[rows, 0:UNITS] = m["gate_w"][...]
-        gate_up[rows, UNITS:] = m["up_w"][...]
+        gate_up[rows, 0:UNITS] = m.gate_w[...]
+        gate_up[rows, UNITS:] = m.up_w[...]
         gate_mate(row).start()
 
-    tokens_two, d_out_ring = m["tokens"], m["d_out_ring"]
-    hidden, d_out = m["hidden"][...].T, m["d_out"][...].T
+    tokens_two, d_out_ring = m.tokens, m.d_out_ring
+    hidden, d_out = m.hidden[...].T, m.d_out[...].T
     tokens_two[0], tokens_two[1] = hidden[:OWN], hidden[OWN:]
     first_half = row == 0
     d_out_ring[0] = jnp.where(first_half, d_out[:OWN], d_out[OWN:])
     d_out_ring[3] = jnp.where(first_half, d_out[OWN:], d_out[:OWN])
-    attn_gain, ffn_gain = m["attn_gain"][...], m["ffn_gain"][...]
+    attn_gain, ffn_gain = m.attn_gain[...], m.ffn_gain[...]
     unit_one, _ = unit_rows(tokens_two[row].astype(F32))
     normed = (unit_one * attn_gain).astype(BF16)
-    m["normed_one"][0] = normed[:, :HALF]
-    m["normed_one"][1] = normed[:, HALF:]
-    first_ring = m["first_ring"]
-    first_ring[0] = m["normed_one"][row]
+    m.normed_one[0] = normed[:, :HALF]
+    m.normed_one[1] = normed[:, HALF:]
+    first_ring = m.first_ring
+    first_ring[0] = m.normed_one[row]
     unit_far, _ = unit_rows(tokens_two[1 - row].astype(F32))
     normed_far = (unit_far * attn_gain).astype(BF16)
     first_ring[3] = jnp.where(first_half, normed_far[:, :HALF], normed_far[:, HALF:])
+
+    gather_w.relay()
 
     for copy in ids_copies:
         copy.wait_recv()
@@ -665,14 +663,14 @@
     earlier = jnp.sum((docs < own_ids).astype(F32), axis=1, keepdims=True)
     start = (low * 2 + s) * 256 + row * OWN
     position = start + lax.broadcasted_iota(jnp.int32, (OWN, 1), 0)
-    angles = (position.astype(F32) - earlier) * m["freq"][...]
+    angles = (position.astype(F32) - earlier) * m.freq[...]
     lane = lax.broadcasted_iota(jnp.int32, (OWN, 128), 1) % HEAD_DIM
     sine = jnp.sin(angles)
-    m["cosine"][...] = jnp.cos(angles)
-    m["sine"][...] = jnp.where(lane < HEAD_DIM // 2, -sine, sine)
+    m.cosine[...] = jnp.cos(angles)
+    m.sine[...] = jnp.where(lane < HEAD_DIM // 2, -sine, sine)
     key_at = lax.broadcasted_iota(jnp.int32, (OWN, KEYS), 1)
     allowed = (own_ids == docs) & (key_at <= position)
-    m["bias"][...] = jnp.where(allowed, 0.0, -jnp.inf).astype(F32)
+    m.bias[...] = jnp.where(allowed, 0.0, -jnp.inf).astype(F32)
 
     @pl.when(active)
     def _():
@@ -693,33 +691,32 @@
     for spread in spreads:
         spread.first()
 
-    gather_w.relay()
-    d_out_copies = [
-        at.send(d_out_ring.at[0], d_out_ring.at[1], up_device),
-        at.send(d_out_ring.at[0], d_out_ring.at[2], down_device),
-    ]
+    gather_w.near()
     for spread in spreads:
         spread.second()
-    gather_w.near()
     gather_w.finish()
     parts = []
     for c in range(4):
-        part = dot_nt(m["normed_one"][0], weights[2 * c]) + dot_nt(m["normed_one"][1], weights[2 * c + 1])
+        part = dot_nt(m.normed_one[0], weights[2 * c]) + dot_nt(m.normed_one[1], weights[2 * c + 1])
         parts.append(part.astype(BF16).astype(F32))
-    cosine, sine = m["cosine"][...], m["sine"][...]
+    cosine, sine = m.cosine[...], m.sine[...]
     k = jnp.concatenate([part[:, 240:320] for part in parts], axis=1)
     v = jnp.concatenate([part[:, 320:400] for part in parts], axis=1)
-    kv = m["kv"]
+    kv = m.kv
     kv[mine] = jnp.concatenate([turn_all(k, cosine, sine), v], axis=1).astype(BF16)
     gather_kv = Gather(at, kv, OWN, OWN // 2, block_of)
     gather_kv.start()
     q = jnp.concatenate([part[:, 0:240] for part in parts], axis=1)
-    m["queries"][...] = turn_all(q, cosine, sine).astype(BF16)
+    m.queries[...] = turn_all(q, cosine, sine).astype(BF16)
     gather_kv.relay()
     for spread in spreads:
         spread.third()
     gather_kv.near()
     gather_kv.finish()
+    d_out_copies = [
+        at.send(d_out_ring.at[0], d_out_ring.at[1], up_device),
+        at.send(d_out_ring.at[0], d_out_ring.at[2], down_device),
+    ]
 
     o_spread.finish()
     o_mate = at.send(o_parts.at[s], o_parts.at[s], mate)
@@ -727,8 +724,8 @@
     for g in range(KV_HEADS):
         key = kv[:, :, g * HEAD_DIM : (g + 1) * HEAD_DIM].reshape(KEYS, HEAD_DIM)
         value = kv[:, :, KVD + g * HEAD_DIM : KVD + (g + 1) * HEAD_DIM].reshape(KEYS, HEAD_DIM)
-        scores = dot_nt(heads_of(m["queries"], g), key) * SCALING
-        scores = scores.reshape(SHARE, OWN, KEYS) + m["bias"][...][None]
+        scores = dot_nt(heads_of(m.queries, g), key) * SCALING
+        scores = scores.reshape(SHARE, OWN, KEYS) + m.bias[...][None]
         top = jnp.max(scores, axis=-1, keepdims=True)
         terms = jnp.exp(scores - top)
         total = jnp.sum(terms, axis=-1, keepdims=True)
@@ -736,11 +733,11 @@
         out = dot(probs, value).astype(BF16)
         for j in range(SHARE):
             head = (g * SHARE + j) * HEAD_DIM
-            m["attn"][:, head : head + HEAD_DIM] = out[j * OWN : (j + 1) * OWN]
-        m["lse"][g] = (top + jnp.log(total)).reshape(SHARE * OWN, 1)
-    attn_halves = m["attn_halves"]
-    attn_halves[0] = m["attn"][:, :HALF]
-    attn_halves[1] = m["attn"][:, HALF:]
+            m.attn[:, head : head + HEAD_DIM] = out[j * OWN : (j + 1) * OWN]
+        m.lse[g] = (top + jnp.log(total)).reshape(SHARE * OWN, 1)
+    attn_halves = m.attn_halves
+    attn_halves[0] = m.attn[:, :HALF]
+    attn_halves[1] = m.attn[:, HALF:]
     o_mate.wait_recv()
 
     def o_block(r, c):
@@ -750,9 +747,9 @@
         dot_nt(attn_halves[0], o_block(0, c)) + dot_nt(attn_halves[1], o_block(1, c)) for c in range(4)
     ]
     middle = tokens_two[row].astype(F32) + jnp.concatenate(attn_out, axis=1)
-    m["middle"][...] = middle
+    m.middle[...] = middle
     unit_two, _ = unit_rows(middle)
-    ring = m["normed_ring"]
+    ring = m.normed_ring
     ring[0] = (unit_two * ffn_gain).astype(BF16)
     gather_n = Gather(at, ring, OWN, OWN // 2)
     gather_n.start()
@@ -770,12 +767,12 @@
     gather_n.relay()
     down_mate.wait_recv()
     for c in range(4):
-        m["down"][c * 240 : (c + 1) * 240] = down_parts[c % 2, :, :, c // 2].reshape(256, UNITS)[0:240]
+        m.down[c * 240 : (c + 1) * 240] = down_parts[c % 2, :, :, c // 2].reshape(256, UNITS)[0:240]
     for copy in d_out_copies:
         copy.wait_recv()
     gate_mate(row).wait_recv()
 
-    ffn_parts, dn_parts = m["ffn_parts"], m["dn_parts"]
+    ffn_parts, dn_parts = m.ffn_parts, m.dn_parts
 
     def feed(p):
         gate_and_up = dot(ring[p], gate_up[...]).astype(BF16)
@@ -783,39 +780,37 @@
         sig = 1.0 / (1.0 + jnp.exp(-gate))
         silu = gate * sig
         unit = (silu * raise_).astype(BF16)
-        m["units"][p] = unit
-        d_unit = dot(d_out_ring[p], m["down"][...])
+        m.units[p] = unit
+        d_unit = dot(d_out_ring[p], m.down[...])
         d_gate = (d_unit * raise_ * sig * (1.0 + gate * (1.0 - sig))).astype(BF16)
         d_up = (d_unit * silu).astype(BF16)
-        m["d_gate_up"][p] = jnp.concatenate([d_gate, d_up], axis=1)
-        d_normed = dot_nt(m["d_gate_up"][p], gate_up[...]).astype(BF16)
+        m.d_gate_up[p] = jnp.concatenate([d_gate, d_up], axis=1)
+        d_normed = dot_nt(m.d_gate_up[p], gate_up[...]).astype(BF16)
         dn_parts[p] = d_normed.reshape(2, OWN // 2, D)
 
     def feed_out(p):
-        ffn_parts[p] = dot_nt(m["units"][p], m["down"][...]).astype(BF16).reshape(2, OWN // 2, D)
-
-    dn = Reduce(at, dn_parts, m["dn_early"], m["dn_sums"], m["dn_landed"])
-    ffn = Reduce(at, ffn_parts, m["ffn_early"], m["ffn_sums"], m["ffn_landed"])
+        ffn_parts[p] = dot_nt(m.units[p], m.down[...]).astype(BF16).reshape(2, OWN // 2, D)
+
+    dn = Reduce(at, dn_parts, m.dn_early, m.dn_sums, m.dn_landed)
+    ffn = Reduce(at, ffn_parts, m.ffn_early, m.ffn_sums, m.ffn_landed)
     feed(0)
     gather_n.near()
     feed(1)
     feed(2)
+    dn.start_near()
     gather_n.finish()
     feed(3)
     dn.start_far()
-    dn.start_near()
     for p in (3, 1, 2):
         feed_out(p)
     dn.middle()
-    ffn.start_far()
-    ffn.start_near()
     feed_out(0)
 
-    halves = m["ffn_halves"]
+    halves = m.ffn_halves
     tokens_n = ring[...].reshape(4 * OWN, D)
-    d_gate_up = m["d_gate_up"][...].reshape(4 * OWN, 2 * UNITS)
+    d_gate_up = m.d_gate_up[...].reshape(4 * OWN, 2 * UNITS)
     tokens_d = d_out_ring[...].reshape(4 * OWN, D)
-    units = m["units"][...].reshape(4 * OWN, UNITS)
+    units = m.units[...].reshape(4 * OWN, UNITS)
     for h in range(2):
         halves[h, 0:HALF, 0 : 2 * UNITS] = dot_tn(tokens_n[:, h * HALF : (h + 1) * HALF], d_gate_up).astype(BF16)
         grad = dot_tn(tokens_d[:, h * HALF : (h + 1) * HALF], units).astype(BF16)
@@ -823,36 +818,28 @@
             halves[h, 32 * i : 32 * i + 16, 2 * UNITS :] = grad[16 * i : 16 * i + 16]
             halves[h, 32 * i + 16 : 32 * i + 32, 2 * UNITS :] = grad[240 + 16 * i : 256 + 16 * i]
         halves[h, HALF:, :] = jnp.zeros((32, 1920), BF16)
-    ffn_pair = at.send(halves.at[1 - s], m["ffn_mate"], mate)
+    ffn_pair = at.send(halves.at[1 - s], m.ffn_mate, mate)
     ffn_collect = Collect(
         at,
-        m["ffn_kept"],
-        m["ffn_far"],
-        m["ffn_pairs"],
-        m["ffn_near"],
-        m["ffn_four"],
-        m["ffn_last"],
-        m["ffn_sum"],
+        m.ffn_kept,
+        m.ffn_far,
+        m.ffn_pairs,
+        m.ffn_near,
+        m.ffn_four,
+        m.ffn_last,
+        m.ffn_sum,
     )
 
     d_normed = dn.finish()
-    ffn.middle()
-    middle = m["middle"][...]
+    middle = m.middle[...]
     unit_two, inverse_two = unit_rows(middle)
     d_middle, ffn_gain_part = norm_back(d_normed, unit_two, inverse_two, ffn_gain)
     d_middle = d_middle + d_out_ring[0].astype(F32)
-    m["d_middle"][...] = d_middle
+    m.d_middle[...] = d_middle
     d_y1 = d_middle.astype(BF16)
-    d_y1_halves, d_y1_ring = m["d_y1_halves"], m["d_y1_ring"]
+    d_y1_halves, d_y1_ring = m.d_y1_halves, m.d_y1_ring
     d_y1_halves[0] = d_y1[:, :HALF]
     d_y1_halves[1] = d_y1[:, HALF:]
-    ffn_pair.wait_recv()
-    for z in range(4):
-        for x in range(4):
-            rows = pl.ds(32 * (4 * z + x), 32)
-            both = halves[s, rows].astype(F32) + m["ffn_mate"][rows].astype(F32)
-            m["ffn_kept"][z, x] = both.astype(BF16).reshape(2, 16, 1920)
-    ffn_collect.start()
     d_attn = [0.0, 0.0]
     for c in range(4):
         for r in range(2):
@@ -860,7 +847,11 @@
     d_attn = jnp.concatenate(d_attn, axis=1).astype(BF16)
 
     up_low, up_row, down_row = 1 - low, at.up // 2, at.down // 2
-    attn_ring, first_send = m["attn_ring"], m["normed_one"]
+    attn_ring, first_send = m.attn_ring, m.normed_one
+    attn_far = Far(at, attn_halves.at[1 - row], attn_ring.at[3], attn_ring.at[3], m.attn_relay)
+    d_y1_far = Far(at, d_y1_halves.at[low], d_y1_ring.at[3], d_y1_ring.at[3], m.d_y1_relay)
+    attn_far.first()
+    d_y1_far.first()
     side_copies = [
         at.send(d_y1_halves.at[up_low], d_y1_ring.at[1], up_device),
         at.send(d_y1_halves.at[up_low], d_y1_ring.at[2], down_device),
@@ -868,23 +859,21 @@
         at.send(attn_halves.at[down_row], attn_ring.at[2], down_device),
         at.send(first_send.at[up_row], first_ring.at[1], up_device),
         at.send(first_send.at[down_row], first_ring.at[2], down_device),
-        at.send(attn_halves.at[1 - row], attn_ring.at[3], far_device),
-        at.send(d_y1_halves.at[low], d_y1_ring.at[3], far_device),
     ]
     attn_ring[0] = attn_halves[row]
     d_y1_ring[0] = d_y1_halves[low]
 
-    d_kv = m["d_kv"]
+    d_kv = m.d_kv
     d_q = []
     for g in range(KV_HEADS):
         own = slice(g * HEAD_DIM, (g + 1) * HEAD_DIM)
         val = slice(KVD + g * HEAD_DIM, KVD + (g + 1) * HEAD_DIM)
         key = kv[:, :, own].reshape(KEYS, HEAD_DIM)
         value = kv[:, :, val].reshape(KEYS, HEAD_DIM)
-        query, d_head = heads_of(m["queries"], g), heads_of(d_attn, g)
+        query, d_head = heads_of(m.queries, g), heads_of(d_attn, g)
         scores = dot_nt(query, key) * SCALING
-        scores = scores.reshape(SHARE, OWN, KEYS) + m["bias"][...][None]
-        probs = jnp.exp(scores.reshape(SHARE * OWN, KEYS) - m["lse"][g])
+        scores = scores.reshape(SHARE, OWN, KEYS) + m.bias[...][None]
+        probs = jnp.exp(scores.reshape(SHARE * OWN, KEYS) - m.lse[g])
         d_probs = dot_nt(d_head, value)
         inner = jnp.sum(probs * d_probs, axis=-1, keepdims=True)
         d_scores = (probs * (d_probs - inner)).astype(BF16)
@@ -892,33 +881,45 @@
         d_q += [d_query[j * OWN : (j + 1) * OWN] for j in range(SHARE)]
         d_kv[:, :, own] = (dot_tn(d_scores, query) * SCALING).astype(BF16).reshape(8, OWN, HEAD_DIM)
         d_kv[:, :, val] = dot_tn(probs.astype(BF16), d_head).astype(BF16).reshape(8, OWN, HEAD_DIM)
-        if g == 2:
+        if g == 0:
+            ffn_pair.wait_recv()
+            for z in range(4):
+                for x in range(4):
+                    rows = pl.ds(32 * (4 * z + x), 32)
+                    both = halves[s, rows].astype(F32) + m.ffn_mate[rows].astype(F32)
+                    m.ffn_kept[z, x] = both.astype(BF16).reshape(2, 16, 1920)
+            ffn_collect.start()
+        if g == 1:
+            attn_far.relay()
+            d_y1_far.relay()
+        if g == 3:
             ffn_collect.middle()
 
     ffn_collect.second()
     kv_copies = []
     order = ((3, at.far), (1, at.down), (2, at.up), (0, y))
     for p, t in order:
-        kv_copies.append(at.send(d_kv.at[block_of(t, 1 - s)], m["kv_mate"].at[p], mate))
-    cosine, sine = m["cosine"][...], -m["sine"][...]
+        kv_copies.append(at.send(d_kv.at[block_of(t, 1 - s)], m.kv_mate.at[p], mate))
+    cosine, sine = m.cosine[...], -m.sine[...]
     d_q = turn_all(jnp.concatenate(d_q, axis=1), cosine, sine).astype(BF16)
-    kv_sum = Reduce(at, m["kv_parts"], m["kv_early"], m["kv_sums"], m["kv_landed"])
+    kv_sum = Reduce(at, m.kv_parts, m.kv_early, m.kv_sums, m.kv_landed)
     for (p, t), copy in zip(order, kv_copies):
         copy.wait_recv()
-        both = d_kv[block_of(t, s)].astype(F32) + m["kv_mate"][p].astype(F32)
-        m["kv_parts"][p] = both.astype(BF16).reshape(2, OWN // 2, 640)
+        both = d_kv[block_of(t, s)].astype(F32) + m.kv_mate[p].astype(F32)
+        m.kv_parts[p] = both.astype(BF16).reshape(2, OWN // 2, 640)
         if p == 3:
             kv_sum.start_far()
         if p == 2:
             kv_sum.start_near()
-    d_q_two, d_q_ring = m["d_q"], m["d_q_ring"]
+    d_q_two, d_q_ring = m.d_q, m.d_q_ring
     d_q_two[0], d_q_two[1] = d_q[:, :HALF], d_q[:, HALF:]
     kv_sum.middle()
     q_copies = [
         at.send(d_q_two.at[up_low], d_q_ring.at[1], up_device),
         at.send(d_q_two.at[up_low], d_q_ring.at[2], down_device),
-        at.send(d_q_two.at[low], d_q_ring.at[3], far_device),
     ]
+    d_q_far = Far(at, d_q_two.at[low], d_q_ring.at[3], d_q_ring.at[3], m.d_q_relay)
+    d_q_far.first()
     d_q_ring[0] = d_q_two[low]
     d_normed_one = [0.0, 0.0]
     for c in range(4):
@@ -926,9 +927,8 @@
             d_normed_one[r] = d_normed_one[r] + dot(d_q[:, c * 240 : (c + 1) * 240], weights[2 * c + r, 0:240])
 
     ffn_collect.reduce()
-    sums, ffn_total = m["ffn_sum"], m["ffn_total"]
+    sums, ffn_total = m.ffn_sum, m.ffn_total
     gate_back_slot, back_slot = at.slots(1), at.slots(2)
-    own_rows = rows_of(dp, 32)
     lanes = pl.ds(2 * UNITS, UNITS)
     owner = low * 2 + s
 
@@ -970,17 +970,19 @@
     d_kv_sum = kv_sum.finish()
     d_k = turn_all(d_kv_sum[:, :KVD], cosine, sine).astype(BF16)
     d_v = d_kv_sum[:, KVD:].astype(BF16)
-    d_kv_own, d_kv_ring = m["d_kv_own"], m["d_kv_ring"]
+    d_kv_own, d_kv_ring = m.d_kv_own, m.d_kv_ring
     for a in range(2):
         d_kv_own[a] = jnp.concatenate(
             [d_k[:, a * 160 : (a + 1) * 160], d_v[:, a * 160 : (a + 1) * 160]], axis=1
         )
+    d_kv_far = Far(at, d_kv_own.at[low], d_kv_ring.at[3], d_kv_ring.at[3], m.d_kv_relay)
+    d_kv_far.first()
     kv_out = [
         at.send(d_kv_own.at[up_low], d_kv_ring.at[1], up_device),
         at.send(d_kv_own.at[up_low], d_kv_ring.at[2], down_device),
-        at.send(d_kv_own.at[low], d_kv_ring.at[3], far_device),
     ]
     d_kv_ring[0] = d_kv_own[low]
+    d_q_far.relay()
 
     for c in range(4):
         piece = jnp.concatenate(
@@ -992,15 +994,21 @@
     d_tokens, attn_gain_part = norm_back(
         jnp.concatenate(d_normed_one, axis=1), unit_one, inverse_one, attn_gain
     )
-    gains = m["gains"]
+    gains = m.gains
     gains[0] = jnp.concatenate([attn_gain_part, ffn_gain_part, jnp.zeros((6, D), F32)], axis=0)
     gain_copies = [
         at.send(gains.at[0], gains.at[1], up_device),
         at.send(gains.at[0], gains.at[2], down_device),
         at.send(gains.at[0], gains.at[3], far_device),
     ]
-    input_grad = m["input_grad"]
-    input_grad[row] = (d_tokens + m["d_middle"][...]).astype(BF16)
+    input_grad = m.input_grad
+    input_grad[row] = (d_tokens + m.d_middle[...]).astype(BF16)
+    input_far = Far(
+        at, input_grad.at[row], input_grad.at[1 - up_row], input_grad.at[1 - down_row], m.input_relay
+    )
+    d_kv_far.relay()
+    ffn.start_far()
+    ffn.start_near()
 
     @pl.when(not_(own_core))
     def _():
@@ -1023,65 +1031,90 @@
 
     for copy in side_copies + q_copies:
         copy.wait_recv()
+    for far in (attn_far, d_y1_far, d_q_far):
+        far.finish()
     first_all = first_ring[...].reshape(4 * OWN, HALF)
     q_grad = dot_tn(first_all, d_q_ring[...].reshape(4 * OWN, HALF)).astype(BF16)
     o_grad = dot_tn(
         attn_ring[...].reshape(4 * OWN, HALF), d_y1_ring[...].reshape(4 * OWN, HALF)
     ).astype(BF16)
-    qo_two = m["qo_two"]
+    qo_two, kv_two = m.qo_two, m.kv_two
     for b in range(2):
         pick = slice(b * 240, (b + 1) * 240)
         qo_two[b, 0:HALF, :] = jnp.concatenate([q_grad[:, pick], o_grad[:, pick]], axis=1)
         qo_two[b, HALF:, :] = jnp.zeros((32, HALF), BF16)
-    qo_ranks = RankSum(
-        at, qo_two, m["qo_mate"], m["qo_kept"], m["qo_ranks"], m["qo_sum"], m["attn_total"]
-    )
-    ffn_spread.second()
-    qo_ranks.start()
+    qo_pair = at.send(qo_two.at[1 - s], m.qo_mate, mate)
+    ffn.middle()
 
     for copy in kv_out + gain_copies:
         copy.wait_recv()
+    d_kv_far.finish()
     kv_grad = dot_tn(first_all, d_kv_ring[...].reshape(4 * OWN, 320)).astype(BF16)
     gain_sum = (gains[0] + gains[1] + gains[2] + gains[3])[0:2].astype(BF16)
     gain_rows = [gain_sum[g : g + 1, p * 160 : (p + 1) * 160] for g in range(2) for p in range(6)]
     gain_block = jnp.concatenate(gain_rows + [jnp.zeros((20, 160), BF16)], axis=0)
-    kv_two = m["kv_two"]
     for b in range(2):
         kv_two[b, 0:HALF, :] = jnp.concatenate(
             [kv_grad[:, b * 80 : (b + 1) * 80], kv_grad[:, 160 + b * 80 : 160 + (b + 1) * 80]], axis=1
         )
         kv_two[b, HALF:, :] = gain_block
-    kv_ranks = RankSum(
-        at, kv_two, m["kv_grad_mate"], m["kv_kept"], m["kv_ranks"], m["kv_sum"], m["kv_total"]
+    kv_pair = at.send(kv_two.at[1 - s], m.kv_grad_mate, mate)
+    ffn_spread.second()
+    attn_kept = m.attn_kept
+    for pair, two, theirs, first in (
+        (qo_pair, qo_two, m.qo_mate, 0),
+        (kv_pair, kv_two, m.kv_grad_mate, HALF),
+    ):
+        pair.wait_recv()
+        both = (two[s].astype(F32) + theirs[...].astype(F32)).astype(BF16)
+        width = both.shape[1]
+        attn_kept[:, :, :, :, first : first + width] = both.reshape(4, 4, 2, 16, width)
+
+    attn_collect = Collect(
+        at,
+        attn_kept,
+        m.attn_far,
+        m.attn_pairs,
+        m.attn_near,
+        m.attn_four,
+        m.attn_last,
+        m.attn_sum,
     )
-    kv_ranks.start()
-    qo_ranks.scatter()
+    attn_collect.start()
+    input_far.first()
     ffn_spread.third()
-    kv_ranks.scatter()
-
-    block_out = m["block_out"]
-    block_out[row] = (m["middle"][...] + ffn.finish()).astype(BF16)
-    out_copies = [
-        at.send(block_out.at[row], block_out.at[row], far_device),
-        at.send(input_grad.at[row], input_grad.at[row], far_device),
-    ]
-
-    qo_ranks.reduce()
-    m["attn_total"][own_rows] = m["qo_sum"][...]
-    qo_ranks.gather()
-    kv_ranks.reduce()
-    m["kv_total"][own_rows] = m["kv_sum"][...]
-    kv_ranks.gather()
-    for copy in out_copies:
-        copy.wait_recv()
+    attn_collect.middle()
+    block_out = m.block_out
+    block_out[row] = (m.middle[...] + ffn.finish()).astype(BF16)
+    block_far = Far(
+        at, block_out.at[row], block_out.at[1 - up_row], block_out.at[1 - down_row], m.block_relay
+    )
+    block_far.first()
+    input_far.relay()
+    attn_collect.second()
+    block_far.relay()
+    attn_collect.reduce()
+    attn_total = m.attn_total
+    attn_total[at.z, at.x] = m.attn_sum[...]
+    attn_spread = Spread(at, attn_total)
+    attn_spread.first()
     ffn_spread.finish()
-    qo_ranks.finish()
-    kv_ranks.finish()
+    leave(3, ffn_total)
+    attn_spread.second()
+    input_far.finish()
+    leave(1, input_grad)
+    block_far.finish()
+    leave(0, block_out)
+    attn_spread.third()
+    attn_spread.finish()
+    leave(2, attn_total)
+    for copy in leaving:
+        copy.wait()
 
     for copy in at.open:
         copy.wait_send()
     gate_mate(row).wait_send()
-    for spread in spreads + (ffn_spread,):
+    for spread in spreads + (ffn_spread, attn_spread):
         spread.drain()
 
     @pl.when(active)
@@ -1112,35 +1145,62 @@
             copy.wait_send()
 
 
+RESULTS = (
+    (D, 2 * OWN), (D, 2 * OWN), (1, D), (HALF, 240), (80, HALF), (80, HALF),
+    (HALF, 240), (1, D), (HALF, UNITS), (HALF, UNITS), (240, 2 * UNITS),
+)
+
+
 def results_kernel(*refs):
-    ins, outs, held, sems = refs[:5], refs[5:16], refs[16:21], refs[21]
+    ins, outs, held, made = refs[:4], refs[4:15], refs[15:19], refs[19:30]
+    in_sem, out_sem = refs[30:]
     copies = [
-        pltpu.make_async_copy(src, dst, sems.at[n]) for n, (src, dst) in enumerate(zip(ins, held))
+        pltpu.make_async_copy(ins[n], held[n], in_sem.at[n]) for n in range(4)
     ]
-    for copy in copies:
+    for n in (3, 0, 1, 2):
+        copies[n].start()
+    block_in, input_in, attn_in, ffn_in = held
+    leaving = []
+
+    def leave(n):
+        copy = pltpu.make_async_copy(made[n], outs[n], out_sem.at[n])
         copy.start()
-    block_in, input_in, attn_in, kv_in, ffn_in = held
-    block, inputs, attn_gain, q_grad, k_grad, v_grad, o_grad, ffn_gain, gate, raise_, down = outs
-    for copy in copies:
-        copy.wait()
-    block[...] = block_in[...].reshape(2 * OWN, D).astype(F32).T
-    inputs[...] = input_in[...].reshape(2 * OWN, D).astype(F32).T
-    q_grad[...] = attn_in[0:HALF, 0:240].astype(F32)
-    o_grad[...] = attn_in[0:HALF, 240:480].astype(F32)
-    kv_grad = kv_in[0:HALF, :].astype(F32).T
-    k_grad[...] = kv_grad[0:80]
-    v_grad[...] = kv_grad[80:160]
-    gains = kv_in[HALF:512, :].astype(F32)
-    for p in range(6):
-        attn_gain[:, p * 160 : (p + 1) * 160] = gains[p : p + 1]
-        ffn_gain[:, p * 160 : (p + 1) * 160] = gains[6 + p : 7 + p]
-    gate[...] = ffn_in[0:CHUNKS, :, :, 0:UNITS].reshape(HALF, UNITS).astype(F32)
-    raise_[...] = ffn_in[0:CHUNKS, :, :, UNITS : 2 * UNITS].reshape(HALF, UNITS).astype(F32)
+        leaving.append(copy)
+
+    copies[3].wait()
+    for n in range(2):
+        made[8 + n][...] = (
+            ffn_in[0:CHUNKS, :, :, n * UNITS : (n + 1) * UNITS].reshape(HALF, UNITS).astype(F32)
+        )
+        leave(8 + n)
     for i in range(CHUNKS):
         for r in range(2):
-            down[16 * i : 16 * i + 16, r * UNITS : (r + 1) * UNITS] = ffn_in[
+            made[10][16 * i : 16 * i + 16, r * UNITS : (r + 1) * UNITS] = ffn_in[
                 i, r, :, 2 * UNITS :
             ].astype(F32)
+    leave(10)
+    for n in range(2):
+        copies[n].wait()
+        made[n][...] = held[n][...].reshape(2 * OWN, D).astype(F32).T
+        leave(n)
+    copies[2].wait()
+    made[3][...] = attn_in[0:CHUNKS, :, :, 0:240].reshape(HALF, 240).astype(F32)
+    leave(3)
+    made[6][...] = attn_in[0:CHUNKS, :, :, 240:480].reshape(HALF, 240).astype(F32)
+    leave(6)
+    kv_grad = attn_in[0:CHUNKS, :, :, 480:640].reshape(HALF, 160).astype(F32).T
+    made[4][...] = kv_grad[0:80]
+    made[5][...] = kv_grad[80:160]
+    leave(4)
+    leave(5)
+    gains = attn_in[CHUNKS, 0, :, 480:640].astype(F32)
+    for p in range(6):
+        made[2][:, p * 160 : (p + 1) * 160] = gains[p : p + 1]
+        made[7][:, p * 160 : (p + 1) * 160] = gains[6 + p : 7 + p]
+    leave(2)
+    leave(7)
+    for copy in leaving:
+        copy.wait()
 
 
 def shards(
@@ -1168,12 +1228,11 @@
         out_shape=[
             jax.ShapeDtypeStruct((2, OWN, D), BF16),
             jax.ShapeDtypeStruct((2, OWN, D), BF16),
-            jax.ShapeDtypeStruct((512, HALF), BF16),
-            jax.ShapeDtypeStruct((512, 160), BF16),
+            jax.ShapeDtypeStruct((4, 4, 2, 16, 640), BF16),
             jax.ShapeDtypeStruct((4, 4, 2, 16, 1920), BF16),
         ],
         in_specs=[local] * len(IN_NAMES),
-        out_specs=[local] * len(OUT_NAMES),
+        out_specs=[pl.BlockSpec(memory_space=pl.ANY)] * 4,
         scratch_shapes=scratch,
         compiler_params=pltpu.CompilerParams(
             collective_id=1, has_side_effects=True, vmem_limit_bytes=60 * 1024 * 1024
@@ -1193,25 +1252,21 @@
         down_weight.T,
         d_out.T,
     )
-    shapes = [
-        (D, 2 * OWN), (D, 2 * OWN), (1, D), (HALF, 240), (80, HALF), (80, HALF),
-        (HALF, 240), (1, D), (HALF, UNITS), (HALF, UNITS), (240, 2 * UNITS),
-    ]
     outs = pl.pallas_call(
         results_kernel,
-        out_shape=[jax.ShapeDtypeStruct(shape, F32) for shape in shapes],
-        in_specs=[pl.BlockSpec(memory_space=pl.ANY)] * len(OUT_NAMES),
-        out_specs=[local] * len(shapes),
+        out_shape=[jax.ShapeDtypeStruct(shape, F32) for shape in RESULTS],
+        in_specs=[pl.BlockSpec(memory_space=pl.ANY)] * 4,
+        out_specs=[pl.BlockSpec(memory_space=pl.ANY)] * len(RESULTS),
         scratch_shapes=[
             pltpu.VMEM((2, OWN, D), BF16),
             pltpu.VMEM((2, OWN, D), BF16),
-            pltpu.VMEM((512, HALF), BF16),
-            pltpu.VMEM((512, 160), BF16),
+            pltpu.VMEM((16, 2, 16, 640), BF16),
             pltpu.VMEM((16, 2, 16, 1920), BF16),
-            pltpu.SemaphoreType.DMA((5,)),
-        ],
+        ]
+        + [pltpu.VMEM(shape, F32) for shape in RESULTS]
+        + [pltpu.SemaphoreType.DMA((4,)), pltpu.SemaphoreType.DMA((len(RESULTS),))],
         compiler_params=pltpu.CompilerParams(vmem_limit_bytes=62 * 1024 * 1024),
-    )(*kept[:4], kept[4].reshape(16, 2, 16, 1920))
+    )(kept[0], kept[1], kept[2].reshape(16, 2, 16, 640), kept[3].reshape(16, 2, 16, 1920))
     turned = (0, 1, 4, 5, 10)
     outs = [out.T if i in turned else out for i, out in enumerate(outs)]
     outs[2], outs[7] = outs[2].reshape(D), outs[7].reshape(D)

time: 158 us -> 151 us (0.956)
  Pallas kernels: 157 us -> 150 us
    pallas_call x1, Pallas kernels: 151 us -> 145 us  [shards(): pl.pallas_call(layer_kernel, out_shape=[jax.ShapeDtypeStruct((2, OWN, D),...]
where the time goes in v2:
time: 151 us
  Pallas kernels  150 us (99%)
    pallas_call x1, Pallas kernels, shards(): pl.pallas_call(layer_kernel, out_shape=[jax.ShapeDtypeStruct((2, OWN, D),...  145 us
    pallas_call x1, Pallas kernels, shards(): pl.pallas_call(results_kernel, out_shape=[jax.ShapeDtypeStruct(shape, F32...  4.61 us

profile of v2, /device:TPU:0, one launch (start us, length us, event | category | flops | bytes accessed | tf_op | source)
XLA Modules:
  0.0 150.6 jit_solution(4550699719337194471)
XLA Ops:
  0.6 145.2 %shard_map.212 = (bf16[2,128,960]{2,1,0:T(8,128)(2,1)}, bf16[2,128,960]{2,1,0:T(8,128)(2,1)}, bf16[4,4,2,16,640]{4,3,2,1,0:T(8,128)(2,1)}, bf16[4,4,2,16,1920]{4,3,2,1,0:T(8,128)(2,1)}) custom-call(bf16[960,256]{1,0:T(8,128)(2,1)} %bitcast.20, s32[1,256]{1,0:T(1,128)} %bitcast.26, f32[1,128]{1,0:T(1,128)} %constant.2.clone.refs_2_, f32[1,960]{1,0:T(1,128)} %bitcast.24, ...), custom_call_target="tpu_custom_call" | custom-call | tf_op jit(solution)/shard_map/pallas_call | solution.py:1226
  145.8 4.6 %shard_map.213 = (f32[960,256]{1,0:T(8,128)}, f32[960,256]{1,0:T(8,128)}, f32[1,960]{1,0:T(1,128)}, f32[480,240]{1,0:T(8,128)}, f32[80,480]{1,0:T(8,128)}, /*ind...) custom-call(bf16[2,128,960]{2,1,0:T(8,128)(2,1)} %get-tuple-element., ...), custom_call_target="tpu_custom_call" | custom-call | tf_op jit(solution)/shard_map/pallas_call | solution.py:1255

commit v3 on v2

--- a/solution.py
+++ b/solution.py
@@ -429,7 +429,8 @@
 IN_NAMES = ("hidden", "ids_in", "freq", "attn_gain", "ffn_gain")
 IN_NAMES += ("q_w", "k_w", "v_w", "o_w", "gate_w", "up_w", "down_w", "d_out")
 SCRATCH = dict(
-    weights=((8, 400, HALF), BF16),
+    wq=((8, 240, HALF), BF16),
+    wkv=((8, 160, HALF), BF16),
     o_parts=((2, 4, 4, 2, 2, 16, HALF), BF16),
     tokens=((2, OWN, D), BF16),
     own_o=((240, HALF), BF16),
@@ -538,10 +539,10 @@
 
     at.greet()
 
-    weights, ids = m.weights, m.ids
-    weights[mine, 0:240] = m.q_w[...].T
-    weights[mine, 240:320] = m.k_w[...]
-    weights[mine, 320:400] = m.v_w[...]
+    wq, wkv, ids = m.wq, m.wkv, m.ids
+    wq[mine] = m.q_w[...].T
+    wkv[mine, 0:80] = m.k_w[...]
+    wkv[mine, 80:160] = m.v_w[...]
     own_row = jnp.where(row == 0, m.ids_in[:, 0:OWN], m.ids_in[:, OWN:]).astype(F32)
     ids[mine] = jnp.broadcast_to(own_row, (16, OWN)).astype(BF16)
     m.own_o[...] = m.o_w[...].T
@@ -596,8 +597,9 @@
         rows = pl.ds(pl.multiple_of(half * HALF, 32), HALF)
         return at.wire(gate_up.at[rows], gate_up.at[rows], mate, gate_mate_slot)
 
-    gather_w = Gather(at, weights, 400, 192, block_of)
-    gather_w.start()
+    gather_kw = Gather(at, wkv, 160, 80, block_of)
+    gather_qw = Gather(at, wq, 240, 112, block_of)
+    gather_kw.start()
     ids_copies = [at.send(ids.at[mine], ids.at[mine], mate)]
     for other in (at.up, at.down, at.far):
         for core in (s, 1 - s):
@@ -643,6 +645,8 @@
     first_half = row == 0
     d_out_ring[0] = jnp.where(first_half, d_out[:OWN], d_out[OWN:])
     d_out_ring[3] = jnp.where(first_half, d_out[OWN:], d_out[:OWN])
+    gather_kw.relay()
+    gather_qw.start()
     attn_gain, ffn_gain = m.attn_gain[...], m.ffn_gain[...]
     unit_one, _ = unit_rows(tokens_two[row].astype(F32))
     normed = (unit_one * attn_gain).astype(BF16)
@@ -654,7 +658,7 @@
     normed_far = (unit_far * attn_gain).astype(BF16)
     first_ring[3] = jnp.where(first_half, normed_far[:, :HALF], normed_far[:, HALF:])
 
-    gather_w.relay()
+    gather_kw.near()
 
     for copy in ids_copies:
         copy.wait_recv()
@@ -691,24 +695,28 @@
     for spread in spreads:
         spread.first()
 
-    gather_w.near()
-    for spread in spreads:
-        spread.second()
-    gather_w.finish()
-    parts = []
-    for c in range(4):
-        part = dot_nt(m.normed_one[0], weights[2 * c]) + dot_nt(m.normed_one[1], weights[2 * c + 1])
-        parts.append(part.astype(BF16).astype(F32))
+    gather_kw.finish()
+
+    def project(buf, c):
+        part = dot_nt(m.normed_one[0], buf[2 * c]) + dot_nt(m.normed_one[1], buf[2 * c + 1])
+        return part.astype(BF16).astype(F32)
+
+    parts = [project(wkv, c) for c in range(4)]
     cosine, sine = m.cosine[...], m.sine[...]
-    k = jnp.concatenate([part[:, 240:320] for part in parts], axis=1)
-    v = jnp.concatenate([part[:, 320:400] for part in parts], axis=1)
+    k = jnp.concatenate([part[:, 0:80] for part in parts], axis=1)
+    v = jnp.concatenate([part[:, 80:160] for part in parts], axis=1)
     kv = m.kv
     kv[mine] = jnp.concatenate([turn_all(k, cosine, sine), v], axis=1).astype(BF16)
     gather_kv = Gather(at, kv, OWN, OWN // 2, block_of)
     gather_kv.start()
-    q = jnp.concatenate([part[:, 0:240] for part in parts], axis=1)
+    gather_qw.relay()
+    for spread in spreads:
+        spread.second()
+    gather_qw.near()
+    gather_kv.relay()
+    gather_qw.finish()
+    q = jnp.concatenate([project(wq, c) for c in range(4)], axis=1)
     m.queries[...] = turn_all(q, cosine, sine).astype(BF16)
-    gather_kv.relay()
     for spread in spreads:
         spread.third()
     gather_kv.near()
@@ -924,7 +932,7 @@
     d_normed_one = [0.0, 0.0]
     for c in range(4):
         for r in range(2):
-            d_normed_one[r] = d_normed_one[r] + dot(d_q[:, c * 240 : (c + 1) * 240], weights[2 * c + r, 0:240])
+            d_normed_one[r] = d_normed_one[r] + dot(d_q[:, c * 240 : (c + 1) * 240], wq[2 * c + r])
 
     ffn_collect.reduce()
     sums, ffn_total = m.ffn_sum, m.ffn_total
@@ -989,7 +997,7 @@
             [d_k[:, c * 80 : (c + 1) * 80], d_v[:, c * 80 : (c + 1) * 80]], axis=1
         )
         for r in range(2):
-            d_normed_one[r] = d_normed_one[r] + dot(piece, weights[2 * c + r, 240:400])
+            d_normed_one[r] = d_normed_one[r] + dot(piece, wkv[2 * c + r])
     unit_one, inverse_one = unit_rows(tokens_two[row].astype(F32))
     d_tokens, attn_gain_part = norm_back(
         jnp.concatenate(d_normed_one, axis=1), unit_one, inverse_one, attn_gain

time: 151 us -> 148 us (0.980)
  Pallas kernels: 150 us -> 147 us
    pallas_call x1, Pallas kernels: 145 us -> 142 us  [shards(): pl.pallas_call(layer_kernel, out_shape=[jax.ShapeDtypeStruct((2, OWN, D),...]
where the time goes in v3:
time: 148 us
  Pallas kernels  147 us (99%)
    pallas_call x1, Pallas kernels, shards(): pl.pallas_call(layer_kernel, out_shape=[jax.ShapeDtypeStruct((2, OWN, D),...  142 us
    pallas_call x1, Pallas kernels, shards(): pl.pallas_call(results_kernel, out_shape=[jax.ShapeDtypeStruct(shape, F32...  4.61 us

profile of v3, /device:TPU:0, one launch (start us, length us, event | category | flops | bytes accessed | tf_op | source)
XLA Modules:
  0.0 147.9 jit_solution(1723098089216810472)
XLA Ops:
  0.6 142.4 %shard_map.212 = (bf16[2,128,960]{2,1,0:T(8,128)(2,1)}, bf16[2,128,960]{2,1,0:T(8,128)(2,1)}, bf16[4,4,2,16,640]{4,3,2,1,0:T(8,128)(2,1)}, bf16[4,4,2,16,1920]{4,3,2,1,0:T(8,128)(2,1)}) custom-call(bf16[960,256]{1,0:T(8,128)(2,1)} %bitcast.20, s32[1,256]{1,0:T(1,128)} %bitcast.26, f32[1,128]{1,0:T(1,128)} %constant.2.clone.refs_2_, f32[1,960]{1,0:T(1,128)} %bitcast.24, ...), custom_call_target="tpu_custom_call" | custom-call | tf_op jit(solution)/shard_map/pallas_call | solution.py:1234
  143.1 4.6 %shard_map.213 = (f32[960,256]{1,0:T(8,128)}, f32[960,256]{1,0:T(8,128)}, f32[1,960]{1,0:T(1,128)}, f32[480,240]{1,0:T(8,128)}, f32[80,480]{1,0:T(8,128)}, /*ind...) custom-call(bf16[2,128,960]{2,1,0:T(8,128)(2,1)} %get-tuple-element., ...), custom_call_target="tpu_custom_call" | custom-call | tf_op jit(solution)/shard_map/pallas_call | solution.py:1263

commit v4 on v3

--- a/solution.py
+++ b/solution.py
@@ -809,10 +809,6 @@
     gather_n.finish()
     feed(3)
     dn.start_far()
-    for p in (3, 1, 2):
-        feed_out(p)
-    dn.middle()
-    feed_out(0)
 
     halves = m.ffn_halves
     tokens_n = ring[...].reshape(4 * OWN, D)
@@ -826,6 +822,8 @@
             halves[h, 32 * i : 32 * i + 16, 2 * UNITS :] = grad[16 * i : 16 * i + 16]
             halves[h, 32 * i + 16 : 32 * i + 32, 2 * UNITS :] = grad[240 + 16 * i : 256 + 16 * i]
         halves[h, HALF:, :] = jnp.zeros((32, 1920), BF16)
+        if h == 0:
+            dn.middle()
     ffn_pair = at.send(halves.at[1 - s], m.ffn_mate, mate)
     ffn_collect = Collect(
         at,
@@ -838,6 +836,8 @@
         m.ffn_sum,
     )
 
+    for p in (3, 1, 2, 0):
+        feed_out(p)
     d_normed = dn.finish()
     middle = m.middle[...]
     unit_two, inverse_two = unit_rows(middle)
@@ -900,14 +900,12 @@
         if g == 1:
             attn_far.relay()
             d_y1_far.relay()
-        if g == 3:
-            ffn_collect.middle()
-
-    ffn_collect.second()
+
     kv_copies = []
     order = ((3, at.far), (1, at.down), (2, at.up), (0, y))
     for p, t in order:
         kv_copies.append(at.send(d_kv.at[block_of(t, 1 - s)], m.kv_mate.at[p], mate))
+    ffn_collect.middle()
     cosine, sine = m.cosine[...], -m.sine[...]
     d_q = turn_all(jnp.concatenate(d_q, axis=1), cosine, sine).astype(BF16)
     kv_sum = Reduce(at, m.kv_parts, m.kv_early, m.kv_sums, m.kv_landed)
@@ -934,7 +932,8 @@
         for r in range(2):
             d_normed_one[r] = d_normed_one[r] + dot(d_q[:, c * 240 : (c + 1) * 240], wq[2 * c + r])
 
-    ffn_collect.reduce()
+    ffn_collect.second()
+
     sums, ffn_total = m.ffn_sum, m.ffn_total
     gate_back_slot, back_slot = at.slots(1), at.slots(2)
     lanes = pl.ds(2 * UNITS, UNITS)
@@ -954,26 +953,6 @@
             back_slot + j,
             back_slot + row,
         )
-
-    @pl.when(own_core)
-    def _():
-        ffn_total[at.z, at.x, :, :, 0 : 2 * UNITS] = sums[:, :, 0 : 2 * UNITS]
-
-    @pl.when(not_(own_core))
-    def _():
-        gate_back().start()
-
-    for j in range(2):
-        here = (owner == y) & (s == j)
-        copy = down_back(j)
-
-        @pl.when(here)
-        def _():
-            ffn_total[at.z, at.x, row, :, 2 * UNITS :] = sums[j, :, 2 * UNITS :]
-
-        @pl.when(not_(here))
-        def _():
-            copy.start()
 
     d_kv_sum = kv_sum.finish()
     d_k = turn_all(d_kv_sum[:, :KVD], cosine, sine).astype(BF16)
@@ -991,6 +970,27 @@
     ]
     d_kv_ring[0] = d_kv_own[low]
     d_q_far.relay()
+    ffn_collect.reduce()
+
+    @pl.when(own_core)
+    def _():
+        ffn_total[at.z, at.x, :, :, 0 : 2 * UNITS] = sums[:, :, 0 : 2 * UNITS]
+
+    @pl.when(not_(own_core))
+    def _():
+        gate_back().start()
+
+    for j in range(2):
+        here = (owner == y) & (s == j)
+        copy = down_back(j)
+
+        @pl.when(here)
+        def _():
+            ffn_total[at.z, at.x, row, :, 2 * UNITS :] = sums[j, :, 2 * UNITS :]
+
+        @pl.when(not_(here))
+        def _():
+            copy.start()
 
     for c in range(4):
         piece = jnp.concatenate(
@@ -1092,6 +1092,7 @@
     input_far.first()
     ffn_spread.third()
     attn_collect.middle()
+    attn_collect.second()
     block_out = m.block_out
     block_out[row] = (m.middle[...] + ffn.finish()).astype(BF16)
     block_far = Far(
@@ -1099,21 +1100,20 @@
     )
     block_far.first()
     input_far.relay()
-    attn_collect.second()
-    block_far.relay()
     attn_collect.reduce()
     attn_total = m.attn_total
     attn_total[at.z, at.x] = m.attn_sum[...]
     attn_spread = Spread(at, attn_total)
     attn_spread.first()
+    block_far.relay()
     ffn_spread.finish()
     leave(3, ffn_total)
     attn_spread.second()
     input_far.finish()
     leave(1, input_grad)
+    attn_spread.third()
     block_far.finish()
     leave(0, block_out)
-    attn_spread.third()
     attn_spread.finish()
     leave(2, attn_total)
     for copy in leaving:

time: 148 us -> 145 us (0.980)
  Pallas kernels: 147 us -> 144 us
    pallas_call x1, Pallas kernels: 142 us -> 139 us  [shards(): pl.pallas_call(layer_kernel, out_shape=[jax.ShapeDtypeStruct((2, OWN, D),...]
where the time goes in v4:
time: 145 us
  Pallas kernels  144 us (99%)
    pallas_call x1, Pallas kernels, shards(): pl.pallas_call(layer_kernel, out_shape=[jax.ShapeDtypeStruct((2, OWN, D),...  139 us
    pallas_call x1, Pallas kernels, shards(): pl.pallas_call(results_kernel, out_shape=[jax.ShapeDtypeStruct(shape, F32...  4.61 us

profile of v4, /device:TPU:0, one launch (start us, length us, event | category | flops | bytes accessed | tf_op | source)
XLA Modules:
  0.0 144.7 jit_solution(17927828084950999051)
XLA Ops:
  0.6 139.2 %shard_map.212 = (bf16[2,128,960]{2,1,0:T(8,128)(2,1)}, bf16[2,128,960]{2,1,0:T(8,128)(2,1)}, bf16[4,4,2,16,640]{4,3,2,1,0:T(8,128)(2,1)}, bf16[4,4,2,16,1920]{4,3,2,1,0:T(8,128)(2,1)}) custom-call(bf16[960,256]{1,0:T(8,128)(2,1)} %bitcast.20, s32[1,256]{1,0:T(1,128)} %bitcast.26, f32[1,128]{1,0:T(1,128)} %constant.2.clone.refs_2_, f32[1,960]{1,0:T(1,128)} %bitcast.24, ...), custom_call_target="tpu_custom_call" | custom-call | tf_op jit(solution)/shard_map/pallas_call | solution.py:1234
  139.9 4.6 %shard_map.213 = (f32[960,256]{1,0:T(8,128)}, f32[960,256]{1,0:T(8,128)}, f32[1,960]{1,0:T(1,128)}, f32[480,240]{1,0:T(8,128)}, f32[80,480]{1,0:T(8,128)}, /*ind...) custom-call(bf16[2,128,960]{2,1,0:T(8,128)(2,1)} %get-tuple-element., ...), custom_call_target="tpu_custom_call" | custom-call | tf_op jit(solution)/shard_map/pallas_call | solution.py:1263

commit v5 on v4

--- a/solution.py
+++ b/solution.py
@@ -427,8 +427,19 @@
 
 
 IN_NAMES = ("hidden", "ids_in", "freq", "attn_gain", "ffn_gain")
+LARGE = ("hidden", "q_w", "k_w", "v_w", "o_w", "gate_w", "up_w", "down_w", "d_out")
 IN_NAMES += ("q_w", "k_w", "v_w", "o_w", "gate_w", "up_w", "down_w", "d_out")
 SCRATCH = dict(
+    hidden=((D, 2 * OWN), BF16),
+    q_w=((HALF, 240), BF16),
+    k_w=((80, HALF), BF16),
+    v_w=((80, HALF), BF16),
+    o_w=((HALF, 240), BF16),
+    gate_w=((HALF, UNITS), BF16),
+    up_w=((HALF, UNITS), BF16),
+    down_w=((240, 2 * UNITS), BF16),
+    d_out=((D, 2 * OWN), BF16),
+    in_sem=pltpu.SemaphoreType.DMA((9,)),
     wq=((8, 240, HALF), BF16),
     wkv=((8, 160, HALF), BF16),
     o_parts=((2, 4, 4, 2, 2, 16, HALF), BF16),
@@ -520,7 +531,9 @@
 def layer_kernel(*refs):
     count = len(IN_NAMES)
     outs, refs = refs[count : count + 4], refs[:count] + refs[count + 4 :]
-    m = types.SimpleNamespace(**dict(zip(IN_NAMES + tuple(SCRATCH), refs)))
+    given = dict(zip(IN_NAMES, refs))
+    held = dict(zip(SCRATCH, refs[count:]))
+    m = types.SimpleNamespace(**{**given, **held})
     leaving = []
 
     def leave(n, src):
@@ -538,14 +551,24 @@
     not_ = jnp.logical_not
 
     at.greet()
+    fetches = {}
+    for n, name in enumerate(("k_w", "v_w", "q_w", "o_w", "down_w", "gate_w", "up_w", "hidden", "d_out")):
+        fetches[name] = pltpu.make_async_copy(given[name], held[name], m.in_sem.at[n])
+        fetches[name].start()
+
+    def fetched(*some):
+        for name in some:
+            fetches[name].wait()
 
     wq, wkv, ids = m.wq, m.wkv, m.ids
+    fetched("k_w", "v_w", "q_w", "o_w")
     wq[mine] = m.q_w[...].T
     wkv[mine, 0:80] = m.k_w[...]
     wkv[mine, 80:160] = m.v_w[...]
     own_row = jnp.where(row == 0, m.ids_in[:, 0:OWN], m.ids_in[:, OWN:]).astype(F32)
     ids[mine] = jnp.broadcast_to(own_row, (16, OWN)).astype(BF16)
     m.own_o[...] = m.o_w[...].T
+    fetched("down_w", "gate_w", "up_w")
     at.meet()
 
     gate_up, o_parts, down_parts = m.gate_up, m.o_parts, m.down_parts
@@ -640,6 +663,7 @@
         gate_mate(row).start()
 
     tokens_two, d_out_ring = m.tokens, m.d_out_ring
+    fetched("hidden", "d_out")
     hidden, d_out = m.hidden[...].T, m.d_out[...].T
     tokens_two[0], tokens_two[1] = hidden[:OWN], hidden[OWN:]
     first_half = row == 0
@@ -1009,14 +1033,7 @@
         at.send(gains.at[0], gains.at[2], down_device),
         at.send(gains.at[0], gains.at[3], far_device),
     ]
-    input_grad = m.input_grad
-    input_grad[row] = (d_tokens + m.d_middle[...]).astype(BF16)
-    input_far = Far(
-        at, input_grad.at[row], input_grad.at[1 - up_row], input_grad.at[1 - down_row], m.input_relay
-    )
     d_kv_far.relay()
-    ffn.start_far()
-    ffn.start_near()
 
     @pl.when(not_(own_core))
     def _():
@@ -1036,6 +1053,14 @@
 
     ffn_spread = Spread(at, ffn_total)
     ffn_spread.first()
+
+    input_grad = m.input_grad
+    input_grad[row] = (d_tokens + m.d_middle[...]).astype(BF16)
+    input_far = Far(
+        at, input_grad.at[row], input_grad.at[1 - up_row], input_grad.at[1 - down_row], m.input_relay
+    )
+    ffn.start_far()
+    ffn.start_near()
 
     for copy in side_copies + q_copies:
         copy.wait_recv()
@@ -1239,7 +1264,7 @@
             jax.ShapeDtypeStruct((4, 4, 2, 16, 640), BF16),
             jax.ShapeDtypeStruct((4, 4, 2, 16, 1920), BF16),
         ],
-        in_specs=[local] * len(IN_NAMES),
+        in_specs=[pl.BlockSpec(memory_space=pl.ANY) if n in LARGE else local for n in IN_NAMES],
         out_specs=[pl.BlockSpec(memory_space=pl.ANY)] * 4,
         scratch_shapes=scratch,
         compiler_params=pltpu.CompilerParams(

time: 145 us -> 144 us (level)
  Pallas kernels: 144 us -> 142 us
    pallas_call x1, Pallas kernels: 139 us -> 138 us  [shards(): pl.pallas_call(layer_kernel, out_shape=[jax.ShapeDtypeStruct((2, OWN, D),...]
where the time goes in v5:
time: 144 us; the launch traced here: 143 us
  Pallas kernels  142 us (99%)
    pallas_call x1, Pallas kernels, shards(): pl.pallas_call(layer_kernel, out_shape=[jax.ShapeDtypeStruct((2, OWN, D),...  138 us
    pallas_call x1, Pallas kernels, shards(): pl.pallas_call(results_kernel, out_shape=[jax.ShapeDtypeStruct(shape, F32...  4.61 us

profile of v5, /device:TPU:0, one launch (start us, length us, event | category | flops | bytes accessed | tf_op | source)
XLA Modules:
  0.0 143.1 jit_solution(15915979301900334062)
XLA Ops:
  0.6 137.7 %shard_map.212 = (bf16[2,128,960]{2,1,0:T(8,128)(2,1)}, bf16[2,128,960]{2,1,0:T(8,128)(2,1)}, bf16[4,4,2,16,640]{4,3,2,1,0:T(8,128)(2,1)}, bf16[4,4,2,16,1920]{4,3,2,1,0:T(8,128)(2,1)}) custom-call(bf16[960,256]{1,0:T(8,128)(2,1)} %bitcast.20, s32[1,256]{1,0:T(1,128)} %bitcast.26, f32[1,128]{1,0:T(1,128)} %constant.2.clone.refs_2_, f32[1,960]{1,0:T(1,128)} %bitcast.24, ...), custom_call_target="tpu_custom_call" | custom-call | tf_op jit(solution)/shard_map/pallas_call | solution.py:1259
  138.3 4.6 %shard_map.213 = (f32[960,256]{1,0:T(8,128)}, f32[960,256]{1,0:T(8,128)}, f32[1,960]{1,0:T(1,128)}, f32[480,240]{1,0:T(8,128)}, f32[80,480]{1,0:T(8,128)}, /*ind...) custom-call(bf16[2,128,960]{2,1,0:T(8,128)(2,1)} %get-tuple-element., ...), custom_call_target="tpu_custom_call" | custom-call | tf_op jit(solution)/shard_map/pallas_call | solution.py:1288
